TPU v7x, 256 devices: a whole 4x4x8 slice. The times are simulated.
256 devices in a mesh: ctx: 8 (over x, core), tp: 32 (over z, y).
Axes of the slice: x: 4, y: 4, z: 8, core: 2. Of those that a mesh axis runs over, the one named last changes fastest.
Arguments:
- tokens: bfloat16 [2048, 8192], P('ctx', 'tp'), may hold values from -6 to 6
- in_weight: bfloat16 [3, 8192, 8192], P(None, 'ctx', 'tp'), may hold values from -0.0625 to 0.0625
- filter_spectrum: float32 [2, 16, 256, 8192], P(None, 'ctx', None, 'tp'), may hold values from -6 to 6
- skip_gain: float32 [8192], P('tp'), may hold values from -4 to 4
- out_weight: bfloat16 [8192, 8192], P(None, 'tp'), may hold values from -0.0625 to 0.0625
Outputs:
- mixed: bfloat16 [2048, 8192], P('ctx', 'tp')
All inputs are finite; a program needn't handle non-finite values.
Results may differ from a plain program's by a relative error of at most 0.007.
Values may be sent and summed in bfloat16 or wider, within the bound.
No kernel may reach another device: no remote copies, remote signals or barrier semaphores. Data moves between devices by JAX's collectives and lax.ppermute only.
A program may use at most 128 MiB of HBM per device.

v0:
```python
import functools
import math

import jax
import jax.numpy as jnp
import ml_dtypes
import numpy as np
from jax import lax
from jax.experimental import pallas as pl
from jax.experimental.pallas import tpu as pltpu
from jax.sharding import Mesh, PartitionSpec as P

NX, NC, NZ, NY = 4, 2, 8, 4
SIZES = dict(x=NX, core=NC, z=NZ, y=NY)
EVERY = ("x", "core", "z", "y")
CTX = ("x", "core")
HALF_CLASSES = 9


def place(x, core, z, y):
    return ((x * NC + core) * NZ + z) * NY + y


MOVE = [
    (place(p, core, 2 * x + f, y), place(x, core, 2 * p + f, y))
    for p in range(4)
    for core in range(2)
    for x in range(4)
    for f in range(2)
    for y in range(4)
]


def shift(values, axis, step):
    n = SIZES[axis]
    return lax.ppermute(values, axis, [(i, (i + step) % n) for i in range(n)])


def near_and_far(block):
    half = block.shape[0] // 2
    plus1, minus1 = shift(block, "z", -1), shift(block, "z", 1)
    plus2, minus2 = shift(block, "z", -2), shift(block, "z", 2)
    plus1, minus1, plus2, minus2 = together(plus1, minus1, plus2, minus2)
    plus3, minus3 = shift(plus2, "z", -1), shift(minus2, "z", 1)
    plus4 = [shift(plus2[:half], "z", -2), shift(minus2[half:], "z", 2)]
    return [block, plus1, plus2, minus1, minus2, plus3, minus3, jnp.concatenate(plus4, 0)]


def together(*values):
    return lax.optimization_barrier(values)


@functools.lru_cache(None)
def tables():
    r = np.arange(256)
    big = 2 * np.pi * (np.outer(r, r) % 256) / 256
    c, s = np.cos(big), np.sin(big)
    both = np.concatenate([c, s], 1).astype(np.float32)
    high = both.astype(ml_dtypes.bfloat16)
    low = (both - high.astype(np.float32)).astype(ml_dtypes.bfloat16)
    j = np.arange(HALF_CLASSES)
    turn = 2 * np.pi * np.outer(j, r) / 4096
    twist = np.concatenate([np.cos(turn), np.sin(turn)], 1).astype(np.float32)
    return high, low, twist[:, None, :]


def small(j, q):
    turn = 2 * math.pi * ((j * q) % 16) / 16
    return round(math.cos(turn), 12), round(math.sin(turn), 12)


def weighted(terms):
    total = None
    for scale, value in terms:
        if scale == 0.0:
            continue
        part = value if scale == 1.0 else -value if scale == -1.0 else scale * value
        total = part if total is None else total + part
    return total


def filter_kernel(
    place_ref, *refs,
):
    (
        skip_ref, sources, out_ref,
        (drive, gate, left, right, h_ref, high_ref, low_ref, twist_ref, piece_ref, sems),
    ) = refs[0], refs[1:9], refs[9], refs[10:]
    targets = [piece_ref.at[k] for k in range(4)] + [h_ref, high_ref, low_ref, twist_ref]
    copies = copy_all(zip(sources, targets), sems)
    tables = copies[4:]
    for copy in copies[:4]:
        copy.wait()

    def transform():
        for part in range(2):
            values = left[part]
            high = values.astype(jnp.bfloat16)
            low = (values - high.astype(jnp.float32)).astype(jnp.bfloat16)
            right[part] = sum(
                jnp.dot(a, b[...], preferred_element_type=jnp.float32)
                for a, b in ((high, high_ref), (high, low_ref), (low, high_ref))
            )

    z, own = place_ref[0], place_ref[2]
    for side, core in enumerate((own, 1 - own)):
        spots = block_spots(core, z)
        for q, (index, column) in zip(spots, ((0, 0), (0, 256), (1, 0), (1, 256))):
            total = piece_ref[2 * side + index, :, column : column + 256]
            gate[q] = total[0:32]
            drive[q] = total[32:64] * total[64:96]
    signal = [drive[q] for q in range(8)]
    for table in tables:
        table.wait()
    for j in range(HALF_CLASSES):
        rows = slice(32 * j, 32 * j + 32)
        cos, sin = twist_ref[j, :, 0:256], twist_ref[j, :, 256:512]
        real = weighted([(small(j, q)[0], signal[q]) for q in range(8)])
        imag = weighted([(-small(j, q)[1], signal[q]) for q in range(8)])
        if imag is None:
            left[0, rows] = real * cos
            left[1, rows] = -real * sin
        else:
            left[0, rows] = real * cos + imag * sin
            left[1, rows] = imag * cos - real * sin
    transform()
    for j in range(HALF_CLASSES):
        rows = slice(32 * j, 32 * j + 32)
        h_real = h_ref[j // 2, 0, j % 2].astype(jnp.float32)
        h_imag = h_ref[j // 2, 1, j % 2].astype(jnp.float32)
        if 0 < j < 8:
            h_real = h_real + h_ref[(16 - j) // 2, 0, j % 2].astype(jnp.float32)
            h_imag = h_imag - h_ref[(16 - j) // 2, 1, j % 2].astype(jnp.float32)
        real = right[0, rows, 0:256] + right[1, rows, 256:512]
        imag = right[1, rows, 0:256] - right[0, rows, 256:512]
        left[0, rows] = real * h_real - imag * h_imag
        left[1, rows] = real * h_imag + imag * h_real
    transform()
    reals, imags = [], []
    for j in range(HALF_CLASSES):
        rows = slice(32 * j, 32 * j + 32)
        cos, sin = twist_ref[j, :, 0:256], twist_ref[j, :, 256:512]
        real = right[0, rows, 0:256] - right[1, rows, 256:512]
        imag = right[1, rows, 0:256] + right[0, rows, 256:512]
        reals.append(real * cos - imag * sin)
        imags.append(real * sin + imag * cos)
    skip = skip_ref[...]
    for q in range(8):
        terms = [(small(j, q)[0], reals[j]) for j in range(HALF_CLASSES)]
        terms += [(-small(j, q)[1], imags[j]) for j in range(HALF_CLASSES)]
        convolved = weighted(terms) * (1.0 / 4096)
        out_ref[q] = (gate[q] * (convolved + skip * drive[q])).astype(out_ref.dtype)


def filtered(where, pieces, spectrum, skip):
    high, low, twist = tables()
    vmem = pl.BlockSpec(memory_space=pltpu.VMEM)
    return pl.pallas_call(
        filter_kernel,
        out_shape=jax.ShapeDtypeStruct((8, 32, 256), jnp.bfloat16),
        in_specs=[pl.BlockSpec(memory_space=pltpu.SMEM)]
        + [vmem]
        + [pl.BlockSpec(memory_space=pl.ANY)] * 8,
        out_specs=vmem,
        scratch_shapes=[
            pltpu.VMEM((8, 32, 256), jnp.float32),
            pltpu.VMEM((8, 32, 256), jnp.float32),
            pltpu.VMEM((2, 32 * HALF_CLASSES, 256), jnp.float32),
            pltpu.VMEM((2, 32 * HALF_CLASSES, 512), jnp.float32),
            pltpu.VMEM((8, 2, 2, 32, 256), jnp.bfloat16),
            pltpu.VMEM((256, 512), jnp.bfloat16),
            pltpu.VMEM((256, 512), jnp.bfloat16),
            pltpu.VMEM((HALF_CLASSES, 1, 512), jnp.float32),
            pltpu.VMEM((4, 96, 512), jnp.float32),
            pltpu.SemaphoreType.DMA((8,)),
        ],
        compiler_params=pltpu.CompilerParams(vmem_limit_bytes=16 * 1024 * 1024),
        cost_estimate=cost(3),
    )(where, skip, *pieces, spectrum, high, low, twist)


def turned_filter(filter_spectrum):
    first = 2 * (NC * lax.axis_index("x") + lax.axis_index("core"))
    eye = np.eye(256, dtype=np.float32)
    own = first + jnp.arange(2, dtype=jnp.int32)
    order = jnp.where((own <= 8)[:, None, None], eye[None], eye[None, :, ::-1])
    turned = jnp.einsum(
        "plgc,lgh->plch",
        filter_spectrum.astype(jnp.bfloat16),
        order.astype(jnp.bfloat16),
        preferred_element_type=jnp.float32,
    ).astype(jnp.bfloat16)
    return turned.reshape(2, 2, 8, 32, 256).transpose(2, 0, 1, 3, 4)


def block_spots(core, z):
    side = jnp.where(z % 2 == 0, 3, 1)
    quarters = [z // 2, z // 2 + side, z // 2 + 4 - side, z // 2 + 2]
    return [2 * (quarter % 4) + core for quarter in quarters]


def cost(microseconds):
    return pl.CostEstimate(
        flops=int(microseconds * 1e9), bytes_accessed=int(microseconds * 3e6), transcendentals=0
    )


def turn_kernel(place_ref, own_ref, sibling_ref, hbm_ref, turned, out_ref, sems):
    z, y, core, x = (place_ref[i] for i in range(4))

    def turn(piece, carry):
        half, k = piece // 4, piece % 4
        own = (z + half) % 2 == core

        def put(ref):
            for part in range(3):
                turned[part] = ref[part, (y + k) % 4].T

        pl.when(own)(lambda: put(own_ref))
        pl.when(jnp.logical_not(own))(lambda: put(sibling_ref))
        columns = pl.ds(pl.multiple_of(256 * k, 256), 256)
        for k_out in range(4):
            for side in range(2):
                start = pl.multiple_of(32 * (2 * ((x + k_out) % 4) + (core + side) % 2), 32)
                for part in range(3):
                    row = 192 * k_out + 96 * side + 32 * part
                    out_ref[half, row : row + 32, columns] = turned[part, pl.ds(start, 32)]
        return carry

    lax.fori_loop(0, 8, turn, 0)
    copies = copy_all([(out_ref.at[half], hbm_ref.at[half]) for half in range(2)], sems)
    for copy in copies:
        copy.wait()


def turned_weight(where, own, sibling):
    vmem = pl.BlockSpec(memory_space=pltpu.VMEM)
    return pl.pallas_call(
        turn_kernel,
        out_shape=jax.ShapeDtypeStruct((2, 768, 1024), jnp.bfloat16),
        in_specs=[pl.BlockSpec(memory_space=pltpu.SMEM), vmem, vmem],
        out_specs=pl.BlockSpec(memory_space=pltpu.HBM),
        scratch_shapes=[
            pltpu.VMEM((3, 256, 256), jnp.bfloat16),
            pltpu.VMEM((2, 768, 1024), jnp.bfloat16),
            pltpu.SemaphoreType.DMA((2,)),
        ],
        compiler_params=pltpu.CompilerParams(vmem_limit_bytes=16 * 1024 * 1024),
        cost_estimate=cost(3),
    )(where, own.reshape(3, 4, 256, 256), sibling.reshape(3, 4, 256, 256))


def copy_all(pairs, sems):
    copies = [
        pltpu.make_async_copy(source, target, sems.at[index])
        for index, (source, target) in enumerate(pairs)
    ]
    for copy in copies:
        copy.start()
    return copies


def join_kernel(*refs):
    parts, out_refs = refs[:4], refs[4:6]
    for k, part in enumerate(parts):
        for half, out_ref in enumerate(out_refs):
            out_ref[:, 256 * k : 256 * k + 256] = part[128 * half : 128 * half + 128]


def joined(parts):
    vmem = pl.BlockSpec(memory_space=pltpu.VMEM)
    return pl.pallas_call(
        join_kernel,
        out_shape=[jax.ShapeDtypeStruct((128, 1024), jnp.bfloat16)] * 2,
        in_specs=[vmem] * 4,
        out_specs=[vmem] * 2,
        cost_estimate=cost(2),
    )(*parts)


def slot_kernel(blocks, count, place_ref, *refs):
    sources, out_refs = refs[: 2 * count + 1], refs[2 * count + 1 : 2 * count + 5]
    unit_ref, weight_ref, sems = refs[2 * count + 5 :]
    pairs = [
        (sources[index], unit_ref.at[index // 2, pl.ds(128 * (index % 2), 128)])
        for index in range(2 * count)
    ]
    copies = copy_all(pairs + [(sources[-1], weight_ref)], sems)
    for copy in copies:
        copy.wait()

    odd = place_ref[0] % 2

    def run(index, carry):
        total = 0.0
        for half in range(2):
            unit = 0
            for number, block in enumerate(blocks):
                even_unit, odd_unit = (
                    [name for name, side in case if side == half][0] for case in block
                )
                unit = jnp.where(index == number, jnp.where(odd, odd_unit, even_unit), unit)
            total += lax.dot_general(
                weight_ref[half], unit_ref[unit], (((1,), (1,)), ((), ())),
                preferred_element_type=jnp.float32,
            )
        columns = pl.ds(pl.multiple_of(256 * index, 256), 256)
        for k, out_ref in enumerate(out_refs):
            rows = slice(192 * k, 192 * k + 192)
            out_ref[:, columns] = total[rows].astype(out_ref.dtype)
        return carry

    lax.fori_loop(0, len(blocks), run, 0)


def slot(where, units, weight, *blocks):
    names = sorted({name for block in blocks for case in block for name, _ in case})
    order = {name: index for index, name in enumerate(names)}
    blocks = [[[(order[name], half) for name, half in case] for case in block] for block in blocks]
    vmem = pl.BlockSpec(memory_space=pltpu.VMEM)
    anywhere = pl.BlockSpec(memory_space=pl.ANY)
    shape = (192, 256 * len(blocks))
    return pl.pallas_call(
        functools.partial(slot_kernel, blocks, len(names)),
        out_shape=[jax.ShapeDtypeStruct(shape, jnp.float32)]
        + [jax.ShapeDtypeStruct(shape, jnp.bfloat16)] * 3,
        in_specs=[pl.BlockSpec(memory_space=pltpu.SMEM)]
        + [anywhere] * (2 * len(names))
        + [pl.BlockSpec(memory_space=pltpu.HBM)],
        out_specs=[vmem] * 4,
        scratch_shapes=[
            pltpu.VMEM((len(names), 256, 1024), jnp.bfloat16),
            pltpu.VMEM((2, 768, 1024), jnp.bfloat16),
            pltpu.SemaphoreType.DMA((2 * len(names) + 1,)),
        ],
        compiler_params=pltpu.CompilerParams(vmem_limit_bytes=16 * 1024 * 1024),
        cost_estimate=cost(3),
    )(where, *[half for name in names for half in units[name]], weight)


def sum_over_x(parts):
    total = parts[0]
    for k in (1, 2, 3):
        total = total + shift(parts[k], "x", k).astype(jnp.float32)
    return total[:96], shift(total[96:], "core", 1)


def mix_kernel(place_ref, *refs):
    blocks, weights, out_ref, ordered = refs[:8], refs[8:10], refs[10], refs[11]
    z, core = place_ref[0], place_ref[2]
    for k, step in enumerate((0, 1, 2, 7, 6, 3, 5, 4)):
        ordered[(z + step + 4 * core) % 8] = blocks[k][...]

    def mix_column(column, carry):
        total = sum(
            jnp.dot(
                ordered[4 * side + row], weights[side][column, row],
                preferred_element_type=jnp.float32,
            )
            for side in range(2)
            for row in range(4)
        )
        out_ref[column] = total.astype(out_ref.dtype)
        return carry

    lax.fori_loop(0, 4, mix_column, 0)


def mix(where, blocks, weights):
    vmem = pl.BlockSpec(memory_space=pltpu.VMEM)
    return pl.pallas_call(
        mix_kernel,
        out_shape=jax.ShapeDtypeStruct((4, 256, 256), jnp.bfloat16),
        in_specs=[pl.BlockSpec(memory_space=pltpu.SMEM)] + [vmem] * 10,
        out_specs=vmem,
        scratch_shapes=[pltpu.VMEM((8, 256, 256), jnp.bfloat16)],
        compiler_params=pltpu.CompilerParams(vmem_limit_bytes=16 * 1024 * 1024),
        cost_estimate=cost(2),
    )(where, *blocks, *weights)


def over_ctx(values):
    return lax.all_to_all(values, CTX, split_axis=0, concat_axis=0, tiled=True)


def shards(tokens, in_weight, filter_spectrum, skip_gain, out_weight):
    x, core = lax.axis_index("x"), lax.axis_index("core")
    z, y = lax.axis_index("z"), lax.axis_index("y")
    where = jnp.stack([z, y, core, x]).astype(jnp.int32)

    block = lax.ppermute(tokens, EVERY, MOVE)
    sibling = shift(in_weight, "core", 1)
    sent_filter = turned_filter(filter_spectrum)
    skip = lax.dynamic_slice_in_dim(skip_gain, 32 * (NC * x + core), 32)[:, None]
    spectrum = over_ctx(sent_filter)
    blocks = [block] + [shift(block, "y", -k) for k in (1, 2, 3)]

    out_weight, _ = together(out_weight, block)
    mine = lax.dynamic_index_in_dim(
        out_weight.reshape(2, 4, 4, 256, 256), core, 0, keepdims=False
    )
    rows = [
        lax.dynamic_index_in_dim(mine, (y + 4 - k) % 4, 1, keepdims=False) for k in range(4)
    ]
    halves = joined(blocks)
    spectrum, halves, rows = together(spectrum, halves, rows)
    units = {"own": halves}
    up, down = ([shift(half, "z", step) for half in halves] for step in (1, -1))
    units["up1"], units["down1"] = up, down
    rows[1] = shift(rows[1], "y", -1)

    weight = turned_weight(where, in_weight, sibling)
    weight, last = together(weight, [up[1], down[1]])
    up, down = (
        [shift(first, "z", step), shift(second, "z", step)]
        for first, second, step in ((up[0], last[0], 1), (down[0], last[1], -1))
    )
    units["up2"], units["down2"] = up, down

    rows[1], rows[3], last = together(rows[1], rows[3], [up[1], down[1]])
    rows[3] = shift(rows[3], "y", -3)
    up, down = (
        [shift(first, "z", step), shift(second, "z", step)]
        for first, second, step in ((up[0], last[0], 1), (down[0], last[1], -1))
    )
    units["up3"], units["down3"] = up, down
    parts = slot(
        where, units, weight,
        [[("own", 0), ("down1", 1)], [("own", 0), ("up1", 1)]],
        [[("up1", 1), ("up2", 0)], [("down1", 1), ("down2", 0)]],
    )
    parts, rows[3], last = together(parts, rows[3], down[1])
    pieces = [sum_over_x(parts)]

    units["across"] = [shift(up[0], "z", 1), shift(last, "z", -1)]
    pieces[0], units["across"] = together(pieces[0], units["across"])
    parts = slot(
        where, units, weight,
        [[("down2", 0), ("down3", 1)], [("up2", 0), ("up3", 1)]],
        [[("up3", 1), ("across", 0)], [("down3", 1), ("across", 0)]],
    )
    rows[2], _ = together(rows[2], parts[0])
    rows[2] = shift(rows[2], "y", -2)
    pieces.append(sum_over_x(parts))
    pieces = [piece[0] for piece in pieces] + [piece[1] for piece in pieces]

    gated = filtered(where, pieces, spectrum, skip)
    gated = over_ctx(gated).reshape(256, 256).T
    rows, _ = together(rows, gated)
    rows = jnp.stack(rows)
    partial = mix(where, near_and_far(gated), [rows, shift(rows, "core", 1)])
    total = partial[0].astype(jnp.float32)
    for k in (1, 2, 3):
        total = total + shift(partial[k], "y", k).astype(jnp.float32)
    return total.astype(jnp.bfloat16)


def solution(mesh):
    fine = Mesh(mesh.devices.reshape(NX, NC, NZ, NY), EVERY)
    tp = ("z", "y")
    placed = (P(CTX, tp), P(None, CTX, tp), P(None, CTX, None, tp), P(tp), P(None, tp))
    return jax.shard_map(
        shards, mesh=fine, in_specs=placed, out_specs=P(CTX, tp), check_vma=False
    )
```

profile of v0, /device:TPU:24, one launch (start us, length us, event | category | flops | bytes accessed | tf_op | source)
XLA Modules:
  0.0 156.9 jit_solution(15359925702788105061)
XLA Ops:
  0.0 1.6 collective-permute-start
  1.6 1.8 %convolution_convert_fusion = bf16[2,256,2,256]{1,3,2,0:T(8,128)(2,1)S(1)} fusion(bf16[256,256]{1,0:T(8,128)(2,1)} %constant.203, bf16[256,256]{1,0:T(8,128)(2,1)} %constant.204, pred[2]{0:T(512)(128)(4,1)S(1)} %add_compare_fusion, f32[2,2,256,256]{3,2,1,0:T(8,128)} %param.12), kind=kOutput, calls=%fused_computation.1 | convolution fusion | flops 134873088 | bytes 1835010 | tf_op jit(solution)/shard_map/plgc,lgh->plch/dot_general | solution.py:187
  4.2 11.8 %all-to-all-start = ((bf16[8,2,2,32,256]{4,3,2,1,0:T(8,128)(2,1)}), bf16[8,2,2,32,256]{4,3,2,1,0:T(8,128)(2,1)S(1)}, u32[]{:S(2)}, u32[]{:S(2)}) async-start(bf16[8,2,2,32,256]{4,3,2,1,0:T(8,128)(2,1)} %bitcast.52), calls=%async_computation | async-start | bytes 1048576 | tf_op jit(solution)/shard_map/all_to_all | solution.py:383
  16.9 0.9 collective-permute-start.2
  17.8 2.2 %collective-permute-start.3 = (bf16[256,256]{1,0:T(8,128)(2,1)S(1)}, bf16[256,256]{1,0:T(8,128)(2,1)}, u32[]{:S(2)}, u32[]{:S(2)}) collective-permute-start(bf16[256,256]{1,0:T(8,128)(2,1)S(1)} %collective-permute-done.refs_0_), channel_id=1, source_target_pairs={{0,1},{1,2},{2,3},{3,0},{4,5},{5,6},{6,7},{7,4},{8,9},{9,10},{10,1... | collective-permute-start | bytes 393224 | tf_op jit(solution)/shard_map/ppermute | solution.py:36
  20.0 2.7 %dynamic-slice_bitcast_fusion = (bf16[4,256,256]{2,1,0:T(8,128)(2,1)}, bf16[4,256,256]{2,1,0:T(8,128)(2,1)S(1)}, bf16[4,256,256]{2,1,0:T(8,128)(2,1)}, bf16[4,256,256]{2,1,0:T(8,128)(2,1)S(1)}) fusion(bf16[2,4,4,256,256]{4,3,2,1,0:T(8,128)(2,1)} %bitcast.61, s32[]{:T(128)S(6)} %select_n.56, s32[]{:T(128)S(6)} %select_n.68, s32[]{:T(128)S(6)} %select_n.65, ...), kind=kLoop, calls=%fused_computation.4 | loop fusion | bytes 4194324 | tf_op jit(solution)/shard_map/jit(dynamic_index_in_dim)/squeeze | solution.py:403
  22.7 3.4 %collective-permute-done.1.refs_1_ = bf16[256,256]{1,0:T(8,128)(2,1)S(1)} collective-permute-done((bf16[256,256]{1,0:T(8,128)(2,1)S(1)}, bf16[256,256]{1,0:T(8,128)(2,1)S(1)}, u32[]{:S(2)}, u32[]{:S(2)}) %collective-permute-start.1) | collective-permute-done | bytes 131104 | tf_op jit(solution)/shard_map/ppermute | solution.py:36
  26.8 1.9 %shard_map.100 = (bf16[128,1024]{1,0:T(8,128)(2,1)}, bf16[128,1024]{1,0:T(8,128)(2,1)}) custom-call(bf16[256,256]{1,0:T(8,128)(2,1)} %copy-done.11, bf16[256,256]{1,0:T(8,128)(2,1)} %copy-done.12, bf16[256,256]{1,0:T(8,128)(2,1)} %copy-done.13, bf16[256,256]{1,0:T(8,128)(2,1)} %collective-permute-done.3.refs_3_), custom_call_target="tpu_custom_call" | custom-call | flops 2000000000 | bytes 6000000 | tf_op jit(solution)/shard_map/pallas_call | solution.py:272
  28.7 3.2 %collective-permute-start.5 = (bf16[128,1024]{1,0:T(8,128)(2,1)}, bf16[128,1024]{1,0:T(8,128)(2,1)S(1)}, u32[]{:S(2)}, u32[]{:S(2)}) collective-permute-start(bf16[128,1024]{1,0:T(8,128)(2,1)} %get-tuple-element.53.refs_5_), channel_id=1, source_target_pairs={{0,28},{4,0},{8,4},{12,8},{16,12},{20,16},{24,20},{28,24},{1,29},{... | collective-permute-start | bytes 786440 | tf_op jit(solution)/shard_map/ppermute | solution.py:36
  31.9 4.9 %collective-permute-start.4 = (bf16[128,1024]{1,0:T(8,128)(2,1)}, bf16[128,1024]{1,0:T(8,128)(2,1)S(1)}, u32[]{:S(2)}, u32[]{:S(2)}) collective-permute-start(bf16[128,1024]{1,0:T(8,128)(2,1)} %get-tuple-element.52.refs_4_), channel_id=1, source_target_pairs={{0,28},{4,0},{8,4},{12,8},{16,12},{20,16},{24,20},{28,24},{1,29},{... | collective-permute-start | bytes 786440 | tf_op jit(solution)/shard_map/ppermute | solution.py:36
  37.5 3.5 %shard_map.101.refs_10_ = bf16[2,768,1024]{2,1,0:T(8,128)(2,1)S(1)} custom-call(s32[4]{0:T(128)S(1)} %pad_add_fusion.place_ref, bf16[3,4,256,256]{3,2,1,0:T(8,128)(2,1)S(1)} %bitcast.58, bf16[3,4,256,256]{3,2,1,0:T(8,128)(2,1)} %bitcast.16.sibling_ref), custom_call_target="tpu_custom_call" | custom-call | flops 3000000000 | bytes 9000000 | tf_op jit(solution)/shard_map/pallas_call | solution.py:238
  41.0 3.3 %collective-permute-done.8.refs_7_ = bf16[128,1024]{1,0:T(8,128)(2,1)S(1)} collective-permute-done((bf16[128,1024]{1,0:T(8,128)(2,1)}, bf16[128,1024]{1,0:T(8,128)(2,1)S(1)}, u32[]{:S(2)}, u32[]{:S(2)}) %collective-permute-start.8) | collective-permute-done | bytes 262176 | tf_op jit(solution)/shard_map/ppermute | solution.py:36
  44.3 3.2 %collective-permute-start.9 = (bf16[128,1024]{1,0:T(8,128)(2,1)S(1)}, bf16[128,1024]{1,0:T(8,128)(2,1)S(1)}, u32[]{:S(2)}, u32[]{:S(2)}) collective-permute-start(bf16[128,1024]{1,0:T(8,128)(2,1)S(1)} %collective-permute-done.5.refs_1_), channel_id=1, source_target_pairs={{0,28},{4,0},{8,4},{12,8},{16,12},{20,16},{24,20},{28,24},{1,29},{... | collective-permute-start | bytes 786440 | tf_op jit(solution)/shard_map/ppermute | solution.py:36
  47.5 2.4 %collective-permute-done.10.refs_6_ = bf16[128,1024]{1,0:T(8,128)(2,1)S(1)} collective-permute-done((bf16[128,1024]{1,0:T(8,128)(2,1)}, bf16[128,1024]{1,0:T(8,128)(2,1)S(1)}, u32[]{:S(2)}, u32[]{:S(2)}) %collective-permute-start.10) | collective-permute-done | bytes 262176 | tf_op jit(solution)/shard_map/ppermute | solution.py:36
  49.9 3.2 %collective-permute-start.6 = (bf16[128,1024]{1,0:T(8,128)(2,1)S(1)}, bf16[128,1024]{1,0:T(8,128)(2,1)S(1)}, u32[]{:S(2)}, u32[]{:S(2)}) collective-permute-start(bf16[128,1024]{1,0:T(8,128)(2,1)S(1)} %collective-permute-done.4.refs_0_), channel_id=1, source_target_pairs={{0,28},{4,0},{8,4},{12,8},{16,12},{20,16},{24,20},{28,24},{1,29},{... | collective-permute-start | bytes 786440 | tf_op jit(solution)/shard_map/ppermute | solution.py:36
  53.1 2.4 %collective-permute-done.12.refs_9_.refs_7_ = bf16[128,1024]{1,0:T(8,128)(2,1)S(1)} collective-permute-done((bf16[128,1024]{1,0:T(8,128)(2,1)S(1)}, bf16[128,1024]{1,0:T(8,128)(2,1)S(1)}, u32[]{:S(2)}, u32[]{:S(2)}) %collective-permute-start.12) | collective-permute-done | bytes 262176 | tf_op jit(solution)/shard_map/ppermute | solution.py:36
  55.5 2.6 %collective-permute-start.14 = (bf16[4,256,256]{2,1,0:T(8,128)(2,1)S(1)}, bf16[4,256,256]{2,1,0:T(8,128)(2,1)S(1)}, u32[]{:S(2)}, u32[]{:S(2)}) collective-permute-start(bf16[4,256,256]{2,1,0:T(8,128)(2,1)S(1)} %copy-done.10), channel_id=1, source_target_pairs={{0,1},{1,2},{2,3},{3,0},{4,5},{5,6},{6,7},{7,4},{8,9},{9,10},{10,1... | collective-permute-start | bytes 1572872 | tf_op jit(solution)/shard_map/ppermute | solution.py:36
  59.0 3.2 %collective-permute-start.15 = (bf16[128,1024]{1,0:T(8,128)(2,1)S(1)}, bf16[128,1024]{1,0:T(8,128)(2,1)S(1)}, u32[]{:S(2)}, u32[]{:S(2)}) collective-permute-start(bf16[128,1024]{1,0:T(8,128)(2,1)S(1)} %collective-permute-done.9.refs_3_), channel_id=1, source_target_pairs={{0,28},{4,0},{8,4},{12,8},{16,12},{20,16},{24,20},{28,24},{1,29},{... | collective-permute-start | bytes 786440 | tf_op jit(solution)/shard_map/ppermute | solution.py:36
  62.3 3.1 %shard_map.102 = (f32[192,512]{1,0:T(8,128)S(1)}, bf16[192,512]{1,0:T(8,128)(2,1)S(1)}, bf16[192,512]{1,0:T(8,128)(2,1)S(1)}, bf16[192,512]{1,0:T(8,128)(2,1)S(1)}) custom-call(s32[4]{0:T(128)S(1)} %pad_add_fusion.place_ref, bf16[128,1024]{1,0:T(8,128)(2,1)S(1)} %collective-permute-done.4.refs_0_, bf16[128,1024]{1,0:T(8,128)(2,1)S(1)} %collective-permute-done.5.refs_1_, ...), custom_call_target="tpu_custom_call" | custom-call | flops 3000000000 | bytes 9000000 | tf_op jit(solution)/shard_map/pallas_call | solution.py:323
  66.4 2.3 %collective-permute-start.17 = (bf16[192,512]{1,0:T(8,128)(2,1)S(1)}, bf16[192,512]{1,0:T(8,128)(2,1)S(1)}, u32[]{:S(2)}, u32[]{:S(2)}) collective-permute-start(bf16[192,512]{1,0:T(8,128)(2,1)S(1)} %get-tuple-element.67), channel_id=1, source_target_pairs={{0,128},{64,192},{128,0},{192,64},{1,129},{65,193},{129,1},{193,65... | collective-permute-start | bytes 589832 | tf_op jit(solution)/shard_map/ppermute | solution.py:36
  68.7 2.6 %collective-permute-start.18 = (bf16[192,512]{1,0:T(8,128)(2,1)S(1)}, bf16[192,512]{1,0:T(8,128)(2,1)S(1)}, u32[]{:S(2)}, u32[]{:S(2)}) collective-permute-start(bf16[192,512]{1,0:T(8,128)(2,1)S(1)} %get-tuple-element.68), channel_id=1, source_target_pairs={{0,192},{64,0},{128,64},{192,128},{1,193},{65,1},{129,65},{193,129... | collective-permute-start | bytes 589832 | tf_op jit(solution)/shard_map/ppermute | solution.py:36
  71.4 3.4 %collective-permute-start.23 = (bf16[128,1024]{1,0:T(8,128)(2,1)S(1)}, bf16[128,1024]{1,0:T(8,128)(2,1)S(1)}, u32[]{:S(2)}, u32[]{:S(2)}) collective-permute-start(bf16[128,1024]{1,0:T(8,128)(2,1)S(1)} %collective-permute-done.6.refs_2_), channel_id=1, source_target_pairs={{0,28},{4,0},{8,4},{12,8},{16,12},{20,16},{24,20},{28,24},{1,29},{... | collective-permute-start | bytes 786440 | tf_op jit(solution)/shard_map/ppermute | solution.py:36
  75.4 3.4 %collective-permute-start.22 = (bf16[128,1024]{1,0:T(8,128)(2,1)S(1)}, bf16[128,1024]{1,0:T(8,128)(2,1)S(1)}, u32[]{:S(2)}, u32[]{:S(2)}) collective-permute-start(bf16[128,1024]{1,0:T(8,128)(2,1)S(1)} %collective-permute-done.15.refs_5_), channel_id=1, source_target_pairs={{0,28},{4,0},{8,4},{12,8},{16,12},{20,16},{24,20},{28,24},{1,29},{... | collective-permute-start | bytes 786440 | tf_op jit(solution)/shard_map/ppermute | solution.py:36
  79.1 3.3 %collective-permute-done.21.refs_0_ = bf16[128,1024]{1,0:T(8,128)(2,1)S(1)} collective-permute-done((bf16[128,1024]{1,0:T(8,128)(2,1)S(1)}, bf16[128,1024]{1,0:T(8,128)(2,1)S(1)}, u32[]{:S(2)}, u32[]{:S(2)}) %collective-permute-start.21) | collective-permute-done | bytes 262176 | tf_op jit(solution)/shard_map/ppermute | solution.py:36
  82.8 2.4 %collective-permute-done.24.refs_9_ = bf16[128,1024]{1,0:T(8,128)(2,1)S(1)} collective-permute-done((bf16[128,1024]{1,0:T(8,128)(2,1)S(1)}, bf16[128,1024]{1,0:T(8,128)(2,1)S(1)}, u32[]{:S(2)}, u32[]{:S(2)}) %collective-permute-start.24) | collective-permute-done | bytes 262176 | tf_op jit(solution)/shard_map/ppermute | solution.py:36
  85.2 3.1 %shard_map.103 = (f32[192,512]{1,0:T(8,128)S(1)}, bf16[192,512]{1,0:T(8,128)(2,1)S(1)}, bf16[192,512]{1,0:T(8,128)(2,1)S(1)}, bf16[192,512]{1,0:T(8,128)(2,1)S(1)}) custom-call(s32[4]{0:T(128)S(1)} %pad_add_fusion.place_ref, bf16[128,1024]{1,0:T(8,128)(2,1)S(1)} %collective-permute-done.21.refs_0_, bf16[128,1024]{1,0:T(8,128)(2,1)S(1)} %collective-permute-done.22.refs_1_, ...), custom_call_target="tpu_custom_call" | custom-call | flops 3000000000 | bytes 9000000 | tf_op jit(solution)/shard_map/pallas_call | solution.py:323
  88.5 1.6 %collective-permute-start.26 = (bf16[192,512]{1,0:T(8,128)(2,1)S(1)}, bf16[192,512]{1,0:T(8,128)(2,1)S(1)}, u32[]{:S(2)}, u32[]{:S(2)}) collective-permute-start(bf16[192,512]{1,0:T(8,128)(2,1)S(1)} %get-tuple-element.76), channel_id=1, source_target_pairs={{0,128},{64,192},{128,0},{192,64},{1,129},{65,193},{129,1},{193,65... | collective-permute-start | bytes 589832 | tf_op jit(solution)/shard_map/ppermute | solution.py:36
  90.1 2.3 %collective-permute-start.27 = (bf16[192,512]{1,0:T(8,128)(2,1)S(1)}, bf16[192,512]{1,0:T(8,128)(2,1)S(1)}, u32[]{:S(2)}, u32[]{:S(2)}) collective-permute-start(bf16[192,512]{1,0:T(8,128)(2,1)S(1)} %get-tuple-element.77), channel_id=1, source_target_pairs={{0,192},{64,0},{128,64},{192,128},{1,193},{65,1},{129,65},{193,129... | collective-permute-start | bytes 589832 | tf_op jit(solution)/shard_map/ppermute | solution.py:36
  92.4 5.1 %collective-permute-done.25 = bf16[192,512]{1,0:T(8,128)(2,1)S(1)} collective-permute-done((bf16[192,512]{1,0:T(8,128)(2,1)S(1)}, bf16[192,512]{1,0:T(8,128)(2,1)S(1)}, u32[]{:S(2)}, u32[]{:S(2)}) %collective-permute-start.25) | collective-permute-done | bytes 196640 | tf_op jit(solution)/shard_map/ppermute | solution.py:36
  98.6 1.2 collective-permute-start.37
  100.0 3.7 %shard_map.104 = bf16[8,32,256]{2,1,0:T(8,128)(2,1)S(1)} custom-call(s32[4]{0:T(128)S(1)} %pad_add_fusion.place_ref, f32[32,1]{1,0:T(8,128)S(1)} %copy.25.refs_0_, f32[96,512]{1,0:T(8,128)S(1)} %get-tuple-element.70.refs_1_, f32[96,512]{1,0:T(8,128)S(1)} %get-tuple-element.101.refs_2_, f32[96,512]{1,0:T(8,128)S(1)} %collective-permute-done.19.refs_3_, ...), custom_call_target="tpu_custom_call" | custom-call | flops 3000000000 | bytes 9000000 | tf_op jit(solution)/shard_map/pallas_call | solution.py:158
  103.8 9.9 %all_to_all.10 = bf16[8,32,256]{2,1,0:T(8,128)(2,1)S(1)} all-to-all(bf16[8,32,256]{2,1,0:T(8,128)(2,1)S(1)} %shard_map.104), channel_id=1, replica_groups=mesh['x'=4,'core'=2,'z'=8,'y'=4] {'x','core'}, dimensions={0} | all-to-all | bytes 262144 | tf_op jit(solution)/shard_map/all_to_all | solution.py:383
  114.5 1.5 pad_maximum_fusion.refs_8_
  116.1 1.6 %collective-permute-start.29 = (bf16[256,256]{1,0:T(8,128)(2,1)S(1)}, bf16[256,256]{1,0:T(8,128)(2,1)S(1)}, u32[]{:S(2)}, u32[]{:S(2)}) collective-permute-start(bf16[256,256]{1,0:T(8,128)(2,1)S(1)} %bitcast.53), channel_id=1, source_target_pairs={{0,28},{4,0},{8,4},{12,8},{16,12},{20,16},{24,20},{28,24},{1,29},{... | collective-permute-start | bytes 393224 | tf_op jit(solution)/shard_map/ppermute | solution.py:36
  118.2 1.5 collective-permute-start.31
  119.7 1.4 collective-permute-start.32
  122.0 5.2 %collective-permute-done.30.refs_3_ = bf16[256,256]{1,0:T(8,128)(2,1)S(1)} collective-permute-done((bf16[256,256]{1,0:T(8,128)(2,1)S(1)}, bf16[256,256]{1,0:T(8,128)(2,1)S(1)}, u32[]{:S(2)}, u32[]{:S(2)}) %collective-permute-start.30) | collective-permute-done | bytes 131104 | tf_op jit(solution)/shard_map/ppermute | solution.py:36
  127.2 2.4 %collective-permute-done.32.refs_4_ = bf16[256,256]{1,0:T(8,128)(2,1)S(1)} collective-permute-done((bf16[256,256]{1,0:T(8,128)(2,1)S(1)}, bf16[256,256]{1,0:T(8,128)(2,1)S(1)}, u32[]{:S(2)}, u32[]{:S(2)}) %collective-permute-start.32) | collective-permute-done | bytes 131104 | tf_op jit(solution)/shard_map/ppermute | solution.py:36
  129.9 2.7 %collective-permute-start.36 = (bf16[128,256]{1,0:T(8,128)(2,1)S(1)}, bf16[128,256]{1,0:T(8,128)(2,1)S(1)}, u32[]{:S(2)}, u32[]{:S(2)}) collective-permute-start(bf16[128,256]{1,0:T(8,128)(2,1)S(1)} %slice.35), channel_id=1, source_target_pairs={{0,8},{4,12},{8,16},{12,20},{16,24},{20,28},{24,0},{28,4},{1,9},{5... | collective-permute-start | bytes 196616 | tf_op jit(solution)/shard_map/ppermute | solution.py:36
  132.6 2.7 %collective-permute-start.33 = (bf16[256,256]{1,0:T(8,128)(2,1)S(1)}, bf16[256,256]{1,0:T(8,128)(2,1)S(1)}, u32[]{:S(2)}, u32[]{:S(2)}) collective-permute-start(bf16[256,256]{1,0:T(8,128)(2,1)S(1)} %collective-permute-done.31.refs_2_), channel_id=1, source_target_pairs={{0,28},{4,0},{8,4},{12,8},{16,12},{20,16},{24,20},{28,24},{1,29},{... | collective-permute-start | bytes 393224 | tf_op jit(solution)/shard_map/ppermute | solution.py:36
  135.6 2.5 %collective-permute-done.36 = bf16[128,256]{1,0:T(8,128)(2,1)S(1)} collective-permute-done((bf16[128,256]{1,0:T(8,128)(2,1)S(1)}, bf16[128,256]{1,0:T(8,128)(2,1)S(1)}, u32[]{:S(2)}, u32[]{:S(2)}) %collective-permute-start.36) | collective-permute-done | bytes 65568 | tf_op jit(solution)/shard_map/ppermute | solution.py:36
  138.3 3.1 %collective-permute-done.34.refs_6_ = bf16[256,256]{1,0:T(8,128)(2,1)S(1)} collective-permute-done((bf16[256,256]{1,0:T(8,128)(2,1)S(1)}, bf16[256,256]{1,0:T(8,128)(2,1)S(1)}, u32[]{:S(2)}, u32[]{:S(2)}) %collective-permute-start.34) | collective-permute-done | bytes 131104 | tf_op jit(solution)/shard_map/ppermute | solution.py:36
  141.5 2.4 %shard_map.105 = bf16[4,256,256]{2,1,0:T(8,128)(2,1)S(1)} custom-call(s32[4]{0:T(128)S(1)} %pad_add_fusion.place_ref, bf16[256,256]{1,0:T(8,128)(2,1)S(1)} %bitcast.57, bf16[256,256]{1,0:T(8,128)(2,1)S(1)} %collective-permute-done.29.refs_1_, bf16[256,256]{1,0:T(8,128)(2,1)S(1)} %collective-permute-done.31.refs_2_, ...), custom_call_target="tpu_custom_call" | custom-call | flops 2000000000 | bytes 6000000 | tf_op jit(solution)/shard_map/pallas_call | solution.py:371
  143.9 4.4 %collective-permute-start.39 = (bf16[256,256]{1,0:T(8,128)(2,1)S(1)}, bf16[256,256]{1,0:T(8,128)(2,1)S(1)}, u32[]{:S(2)}, u32[]{:S(2)}) collective-permute-start(bf16[256,256]{1,0:T(8,128)(2,1)S(1)} %get-tuple-element.97), channel_id=1, source_target_pairs={{0,1},{1,2},{2,3},{3,0},{4,5},{5,6},{6,7},{7,4},{8,9},{9,10},{10,1... | collective-permute-start | bytes 393224 | tf_op jit(solution)/shard_map/ppermute | solution.py:36
  148.3 1.0 collective-permute-start.40
  149.4 2.9 %collective-permute-done.39 = bf16[256,256]{1,0:T(8,128)(2,1)S(1)} collective-permute-done((bf16[256,256]{1,0:T(8,128)(2,1)S(1)}, bf16[256,256]{1,0:T(8,128)(2,1)S(1)}, u32[]{:S(2)}, u32[]{:S(2)}) %collective-permute-start.39) | collective-permute-done | bytes 131104 | tf_op jit(solution)/shard_map/ppermute | solution.py:36
  152.3 2.6 %collective-permute-done.40 = bf16[256,256]{1,0:T(8,128)(2,1)S(1)} collective-permute-done((bf16[256,256]{1,0:T(8,128)(2,1)S(1)}, bf16[256,256]{1,0:T(8,128)(2,1)S(1)}, u32[]{:S(2)}, u32[]{:S(2)}) %collective-permute-start.40) | collective-permute-done | bytes 131104 | tf_op jit(solution)/shard_map/ppermute | solution.py:36
  154.9 1.3 collective-permute-done.41
  (91 shorter events, 11.7 us)
Async XLA Ops:
  0.0 99.7 %copy-start = (f32[256]{0:T(256)S(1)}, f32[256]{0:T(256)}, u32[]{:S(2)}) copy-start(f32[256]{0:T(256)} %param.13) | copy-start | bytes 3076
  0.0 36.8 %collective-permute-start.7 = (bf16[3,1024,256]{2,1,0:T(8,128)(2,1)}, bf16[3,1024,256]{2,1,0:T(8,128)(2,1)}, u32[]{:S(2)}, u32[]{:S(2)}) collective-permute-start(bf16[3,1024,256]{2,1,0:T(8,128)(2,1)} %param.11), channel_id=1, source_target_pairs={{0,32},{32,0},{1,33},{33,1},{2,34},{34,2},{3,35},{35,3},{4,36},{36... | collective-permute-start | bytes 4718600 | tf_op jit(solution)/shard_map/ppermute | solution.py:36
  0.0 16.1 %collective-permute-start = (bf16[256,256]{1,0:T(8,128)(2,1)}, bf16[256,256]{1,0:T(8,128)(2,1)S(1)}, u32[]{:S(2)}, u32[]{:S(2)}) collective-permute-start(bf16[256,256]{1,0:T(8,128)(2,1)} %param.10), channel_id=1, source_target_pairs={{0,0},{1,1},{2,2},{3,3},{4,4},{5,5},{6,6},{7,7},{8,64},{9,65},{10,... | collective-permute-start | bytes 393224 | tf_op jit(solution)/shard_map/ppermute | solution.py:391
  4.2 24.5 %all-to-all-start = ((bf16[8,2,2,32,256]{4,3,2,1,0:T(8,128)(2,1)}), bf16[8,2,2,32,256]{4,3,2,1,0:T(8,128)(2,1)S(1)}, u32[]{:S(2)}, u32[]{:S(2)}) async-start(bf16[8,2,2,32,256]{4,3,2,1,0:T(8,128)(2,1)} %bitcast.52), calls=%async_computation | async-start | bytes 1048576 | tf_op jit(solution)/shard_map/all_to_all | solution.py:383
  16.1 10.0 %collective-permute-start.1 = (bf16[256,256]{1,0:T(8,128)(2,1)S(1)}, bf16[256,256]{1,0:T(8,128)(2,1)S(1)}, u32[]{:S(2)}, u32[]{:S(2)}) collective-permute-start(bf16[256,256]{1,0:T(8,128)(2,1)S(1)} %collective-permute-done.refs_0_), channel_id=1, source_target_pairs={{0,3},{1,0},{2,1},{3,2},{4,7},{5,4},{6,5},{7,6},{8,11},{9,8},{10,9... | collective-permute-start | bytes 393224 | tf_op jit(solution)/shard_map/ppermute | solution.py:36
  16.9 9.2 %collective-permute-start.2 = (bf16[256,256]{1,0:T(8,128)(2,1)S(1)}, bf16[256,256]{1,0:T(8,128)(2,1)S(1)}, u32[]{:S(2)}, u32[]{:S(2)}) collective-permute-start(bf16[256,256]{1,0:T(8,128)(2,1)S(1)} %collective-permute-done.refs_0_), channel_id=1, source_target_pairs={{0,2},{1,3},{2,0},{3,1},{4,6},{5,7},{6,4},{7,5},{8,10},{9,11},{10,... | collective-permute-start | bytes 393224 | tf_op jit(solution)/shard_map/ppermute | solution.py:36
  17.8 9.0 %collective-permute-start.3 = (bf16[256,256]{1,0:T(8,128)(2,1)S(1)}, bf16[256,256]{1,0:T(8,128)(2,1)}, u32[]{:S(2)}, u32[]{:S(2)}) collective-permute-start(bf16[256,256]{1,0:T(8,128)(2,1)S(1)} %collective-permute-done.refs_0_), channel_id=1, source_target_pairs={{0,1},{1,2},{2,3},{3,0},{4,5},{5,6},{6,7},{7,4},{8,9},{9,10},{10,1... | collective-permute-start | bytes 393224 | tf_op jit(solution)/shard_map/ppermute | solution.py:36
  28.7 12.3 %collective-permute-start.5 = (bf16[128,1024]{1,0:T(8,128)(2,1)}, bf16[128,1024]{1,0:T(8,128)(2,1)S(1)}, u32[]{:S(2)}, u32[]{:S(2)}) collective-permute-start(bf16[128,1024]{1,0:T(8,128)(2,1)} %get-tuple-element.53.refs_5_), channel_id=1, source_target_pairs={{0,28},{4,0},{8,4},{12,8},{16,12},{20,16},{24,20},{28,24},{1,29},{... | collective-permute-start | bytes 786440 | tf_op jit(solution)/shard_map/ppermute | solution.py:36
  31.9 12.4 %collective-permute-start.8 = (bf16[128,1024]{1,0:T(8,128)(2,1)}, bf16[128,1024]{1,0:T(8,128)(2,1)S(1)}, u32[]{:S(2)}, u32[]{:S(2)}) collective-permute-start(bf16[128,1024]{1,0:T(8,128)(2,1)} %get-tuple-element.53.refs_5_), channel_id=1, source_target_pairs={{0,4},{4,8},{8,12},{12,16},{16,20},{20,24},{24,28},{28,0},{1,5},{5... | collective-permute-start | bytes 786440 | tf_op jit(solution)/shard_map/ppermute | solution.py:36
  31.9 18.0 %collective-permute-start.10 = (bf16[128,1024]{1,0:T(8,128)(2,1)}, bf16[128,1024]{1,0:T(8,128)(2,1)S(1)}, u32[]{:S(2)}, u32[]{:S(2)}) collective-permute-start(bf16[128,1024]{1,0:T(8,128)(2,1)} %get-tuple-element.52.refs_4_), channel_id=1, source_target_pairs={{0,4},{4,8},{8,12},{12,16},{16,20},{20,24},{24,28},{28,0},{1,5},{5... | collective-permute-start | bytes 786440 | tf_op jit(solution)/shard_map/ppermute | solution.py:36
  31.9 18.0 %collective-permute-start.4 = (bf16[128,1024]{1,0:T(8,128)(2,1)}, bf16[128,1024]{1,0:T(8,128)(2,1)S(1)}, u32[]{:S(2)}, u32[]{:S(2)}) collective-permute-start(bf16[128,1024]{1,0:T(8,128)(2,1)} %get-tuple-element.52.refs_4_), channel_id=1, source_target_pairs={{0,28},{4,0},{8,4},{12,8},{16,12},{20,16},{24,20},{28,24},{1,29},{... | collective-permute-start | bytes 786440 | tf_op jit(solution)/shard_map/ppermute | solution.py:36
  36.8 16.3 %collective-permute-start.13 = (bf16[4,256,256]{2,1,0:T(8,128)(2,1)}, bf16[4,256,256]{2,1,0:T(8,128)(2,1)S(1)}, u32[]{:S(2)}, u32[]{:S(2)}) collective-permute-start(bf16[4,256,256]{2,1,0:T(8,128)(2,1)} %get-tuple-element.61), channel_id=1, source_target_pairs={{0,3},{1,0},{2,1},{3,2},{4,7},{5,4},{6,5},{7,6},{8,11},{9,8},{10,9... | collective-permute-start | bytes 1572872 | tf_op jit(solution)/shard_map/ppermute | solution.py:36
  37.5 18.1 %copy-start.10 = (bf16[4,256,256]{2,1,0:T(8,128)(2,1)S(1)}, bf16[4,256,256]{2,1,0:T(8,128)(2,1)}, u32[]{:S(2)}) copy-start(bf16[4,256,256]{2,1,0:T(8,128)(2,1)} %get-tuple-element.63) | copy-start | bytes 1572868
  37.5 24.8 %copy-start.2 = (bf16[128,1024]{1,0:T(8,128)(2,1)S(1)}, bf16[128,1024]{1,0:T(8,128)(2,1)}, u32[]{:S(2)}) copy-start(bf16[128,1024]{1,0:T(8,128)(2,1)} %get-tuple-element.52.refs_4_) | copy-start | bytes 786436
  37.5 24.8 %copy-start.3 = (bf16[128,1024]{1,0:T(8,128)(2,1)S(1)}, bf16[128,1024]{1,0:T(8,128)(2,1)}, u32[]{:S(2)}) copy-start(bf16[128,1024]{1,0:T(8,128)(2,1)} %get-tuple-element.53.refs_5_) | copy-start | bytes 786436
  44.3 11.2 %collective-permute-start.12 = (bf16[128,1024]{1,0:T(8,128)(2,1)S(1)}, bf16[128,1024]{1,0:T(8,128)(2,1)S(1)}, u32[]{:S(2)}, u32[]{:S(2)}) collective-permute-start(bf16[128,1024]{1,0:T(8,128)(2,1)S(1)} %collective-permute-done.8.refs_7_), channel_id=1, source_target_pairs={{0,4},{4,8},{8,12},{12,16},{16,20},{20,24},{24,28},{28,0},{1,5},{5... | collective-permute-start | bytes 786440 | tf_op jit(solution)/shard_map/ppermute | solution.py:36
  44.3 11.2 %collective-permute-start.9 = (bf16[128,1024]{1,0:T(8,128)(2,1)S(1)}, bf16[128,1024]{1,0:T(8,128)(2,1)S(1)}, u32[]{:S(2)}, u32[]{:S(2)}) collective-permute-start(bf16[128,1024]{1,0:T(8,128)(2,1)S(1)} %collective-permute-done.5.refs_1_), channel_id=1, source_target_pairs={{0,28},{4,0},{8,4},{12,8},{16,12},{20,16},{24,20},{28,24},{1,29},{... | collective-permute-start | bytes 786440 | tf_op jit(solution)/shard_map/ppermute | solution.py:36
  49.9 9.1 %collective-permute-start.11 = (bf16[128,1024]{1,0:T(8,128)(2,1)S(1)}, bf16[128,1024]{1,0:T(8,128)(2,1)S(1)}, u32[]{:S(2)}, u32[]{:S(2)}) collective-permute-start(bf16[128,1024]{1,0:T(8,128)(2,1)S(1)} %collective-permute-done.10.refs_6_), channel_id=1, source_target_pairs={{0,4},{4,8},{8,12},{12,16},{16,20},{20,24},{24,28},{28,0},{1,5},{5... | collective-permute-start | bytes 786440 | tf_op jit(solution)/shard_map/ppermute | solution.py:36
  49.9 12.4 %collective-permute-start.6 = (bf16[128,1024]{1,0:T(8,128)(2,1)S(1)}, bf16[128,1024]{1,0:T(8,128)(2,1)S(1)}, u32[]{:S(2)}, u32[]{:S(2)}) collective-permute-start(bf16[128,1024]{1,0:T(8,128)(2,1)S(1)} %collective-permute-done.4.refs_0_), channel_id=1, source_target_pairs={{0,28},{4,0},{8,4},{12,8},{16,12},{20,16},{24,20},{28,24},{1,29},{... | collective-permute-start | bytes 786440 | tf_op jit(solution)/shard_map/ppermute | solution.py:36
  55.5 10.9 %collective-permute-start.14 = (bf16[4,256,256]{2,1,0:T(8,128)(2,1)S(1)}, bf16[4,256,256]{2,1,0:T(8,128)(2,1)S(1)}, u32[]{:S(2)}, u32[]{:S(2)}) collective-permute-start(bf16[4,256,256]{2,1,0:T(8,128)(2,1)S(1)} %copy-done.10), channel_id=1, source_target_pairs={{0,1},{1,2},{2,3},{3,0},{4,5},{5,6},{6,7},{7,4},{8,9},{9,10},{10,1... | collective-permute-start | bytes 1572872 | tf_op jit(solution)/shard_map/ppermute | solution.py:36
  59.0 15.8 %collective-permute-start.20 = (bf16[128,1024]{1,0:T(8,128)(2,1)S(1)}, bf16[128,1024]{1,0:T(8,128)(2,1)S(1)}, u32[]{:S(2)}, u32[]{:S(2)}) collective-permute-start(bf16[128,1024]{1,0:T(8,128)(2,1)S(1)} %collective-permute-done.11.refs_8_.refs_6_), channel_id=1, source_target_pairs={{0,4},{4,8},{8,12},{12,16},{16,20},{20,24},{24,28},{28,0},{1,5},{5... | collective-permute-start | bytes 786440 | tf_op jit(solution)/shard_map/ppermute | solution.py:36
  59.0 7.1 %collective-permute-start.15 = (bf16[128,1024]{1,0:T(8,128)(2,1)S(1)}, bf16[128,1024]{1,0:T(8,128)(2,1)S(1)}, u32[]{:S(2)}, u32[]{:S(2)}) collective-permute-start(bf16[128,1024]{1,0:T(8,128)(2,1)S(1)} %collective-permute-done.9.refs_3_), channel_id=1, source_target_pairs={{0,28},{4,0},{8,4},{12,8},{16,12},{20,16},{24,20},{28,24},{1,29},{... | collective-permute-start | bytes 786440 | tf_op jit(solution)/shard_map/ppermute | solution.py:36
  66.4 21.9 %copy-start.9 = (bf16[4,256,256]{2,1,0:T(8,128)(2,1)}, bf16[4,256,256]{2,1,0:T(8,128)(2,1)S(1)}, u32[]{:S(2)}) copy-start(bf16[4,256,256]{2,1,0:T(8,128)(2,1)S(1)} %collective-permute-done.14) | copy-start | bytes 1572868
  66.4 9.0 %collective-permute-start.16 = (bf16[192,512]{1,0:T(8,128)(2,1)S(1)}, bf16[192,512]{1,0:T(8,128)(2,1)S(1)}, u32[]{:S(2)}, u32[]{:S(2)}) collective-permute-start(bf16[192,512]{1,0:T(8,128)(2,1)S(1)} %get-tuple-element.66), channel_id=1, source_target_pairs={{0,64},{64,128},{128,192},{192,0},{1,65},{65,129},{129,193},{193,1... | collective-permute-start | bytes 589832 | tf_op jit(solution)/shard_map/ppermute | solution.py:36
  66.4 9.0 %collective-permute-start.17 = (bf16[192,512]{1,0:T(8,128)(2,1)S(1)}, bf16[192,512]{1,0:T(8,128)(2,1)S(1)}, u32[]{:S(2)}, u32[]{:S(2)}) collective-permute-start(bf16[192,512]{1,0:T(8,128)(2,1)S(1)} %get-tuple-element.67), channel_id=1, source_target_pairs={{0,128},{64,192},{128,0},{192,64},{1,129},{65,193},{129,1},{193,65... | collective-permute-start | bytes 589832 | tf_op jit(solution)/shard_map/ppermute | solution.py:36
  68.7 10.1 %collective-permute-start.18 = (bf16[192,512]{1,0:T(8,128)(2,1)S(1)}, bf16[192,512]{1,0:T(8,128)(2,1)S(1)}, u32[]{:S(2)}, u32[]{:S(2)}) collective-permute-start(bf16[192,512]{1,0:T(8,128)(2,1)S(1)} %get-tuple-element.68), channel_id=1, source_target_pairs={{0,192},{64,0},{128,64},{192,128},{1,193},{65,1},{129,65},{193,129... | collective-permute-start | bytes 589832 | tf_op jit(solution)/shard_map/ppermute | solution.py:36
  71.4 11.4 %collective-permute-start.23 = (bf16[128,1024]{1,0:T(8,128)(2,1)S(1)}, bf16[128,1024]{1,0:T(8,128)(2,1)S(1)}, u32[]{:S(2)}, u32[]{:S(2)}) collective-permute-start(bf16[128,1024]{1,0:T(8,128)(2,1)S(1)} %collective-permute-done.6.refs_2_), channel_id=1, source_target_pairs={{0,28},{4,0},{8,4},{12,8},{16,12},{20,16},{24,20},{28,24},{1,29},{... | collective-permute-start | bytes 786440 | tf_op jit(solution)/shard_map/ppermute | solution.py:36
  74.8 7.6 %collective-permute-start.21 = (bf16[128,1024]{1,0:T(8,128)(2,1)S(1)}, bf16[128,1024]{1,0:T(8,128)(2,1)S(1)}, u32[]{:S(2)}, u32[]{:S(2)}) collective-permute-start(bf16[128,1024]{1,0:T(8,128)(2,1)S(1)} %collective-permute-done.20.refs_8_), channel_id=1, source_target_pairs={{0,4},{4,8},{8,12},{12,16},{16,20},{20,24},{24,28},{28,0},{1,5},{5... | collective-permute-start | bytes 786440 | tf_op jit(solution)/shard_map/ppermute | solution.py:36
  75.4 9.8 %collective-permute-start.24 = (bf16[128,1024]{1,0:T(8,128)(2,1)S(1)}, bf16[128,1024]{1,0:T(8,128)(2,1)S(1)}, u32[]{:S(2)}, u32[]{:S(2)}) collective-permute-start(bf16[128,1024]{1,0:T(8,128)(2,1)S(1)} %collective-permute-done.12.refs_9_.refs_7_), channel_id=1, source_target_pairs={{0,4},{4,8},{8,12},{12,16},{16,20},{20,24},{24,28},{28,0},{1,5},{5... | collective-permute-start | bytes 786440 | tf_op jit(solution)/shard_map/ppermute | solution.py:36
  75.4 7.4 %collective-permute-start.22 = (bf16[128,1024]{1,0:T(8,128)(2,1)S(1)}, bf16[128,1024]{1,0:T(8,128)(2,1)S(1)}, u32[]{:S(2)}, u32[]{:S(2)}) collective-permute-start(bf16[128,1024]{1,0:T(8,128)(2,1)S(1)} %collective-permute-done.15.refs_5_), channel_id=1, source_target_pairs={{0,28},{4,0},{8,4},{12,8},{16,12},{20,16},{24,20},{28,24},{1,29},{... | collective-permute-start | bytes 786440 | tf_op jit(solution)/shard_map/ppermute | solution.py:36
  79.0 3.8 %collective-permute-start.19 = (f32[96,512]{1,0:T(8,128)S(1)}, f32[96,512]{1,0:T(8,128)S(1)}, u32[]{:S(2)}, u32[]{:S(2)}) collective-permute-start(f32[96,512]{1,0:T(8,128)S(1)} %get-tuple-element.102), channel_id=1, source_target_pairs={{0,32},{32,0},{1,33},{33,1},{2,34},{34,2},{3,35},{35,3},{4,36},{36... | collective-permute-start | bytes 589832 | tf_op jit(solution)/shard_map/ppermute | solution.py:36
  88.4 9.1 %collective-permute-start.25 = (bf16[192,512]{1,0:T(8,128)(2,1)S(1)}, bf16[192,512]{1,0:T(8,128)(2,1)S(1)}, u32[]{:S(2)}, u32[]{:S(2)}) collective-permute-start(bf16[192,512]{1,0:T(8,128)(2,1)S(1)} %get-tuple-element.75), channel_id=1, source_target_pairs={{0,64},{64,128},{128,192},{192,0},{1,65},{65,129},{129,193},{193,1... | collective-permute-start | bytes 589832 | tf_op jit(solution)/shard_map/ppermute | solution.py:36
  88.5 9.0 %collective-permute-start.26 = (bf16[192,512]{1,0:T(8,128)(2,1)S(1)}, bf16[192,512]{1,0:T(8,128)(2,1)S(1)}, u32[]{:S(2)}, u32[]{:S(2)}) collective-permute-start(bf16[192,512]{1,0:T(8,128)(2,1)S(1)} %get-tuple-element.76), channel_id=1, source_target_pairs={{0,128},{64,192},{128,0},{192,64},{1,129},{65,193},{129,1},{193,65... | collective-permute-start | bytes 589832 | tf_op jit(solution)/shard_map/ppermute | solution.py:36
  90.1 8.2 %collective-permute-start.27 = (bf16[192,512]{1,0:T(8,128)(2,1)S(1)}, bf16[192,512]{1,0:T(8,128)(2,1)S(1)}, u32[]{:S(2)}, u32[]{:S(2)}) collective-permute-start(bf16[192,512]{1,0:T(8,128)(2,1)S(1)} %get-tuple-element.77), channel_id=1, source_target_pairs={{0,192},{64,0},{128,64},{192,128},{1,193},{65,1},{129,65},{193,129... | collective-permute-start | bytes 589832 | tf_op jit(solution)/shard_map/ppermute | solution.py:36
  98.5 1.5 collective-permute-start.28
  98.6 15.9 %collective-permute-start.37 = (bf16[4,256,256]{2,1,0:T(8,128)(2,1)S(1)}, bf16[4,256,256]{2,1,0:T(8,128)(2,1)}, u32[]{:S(2)}, u32[]{:S(2)}) collective-permute-start(bf16[4,256,256]{2,1,0:T(8,128)(2,1)S(1)} %get-tuple-element.87), channel_id=1, source_target_pairs={{0,2},{1,3},{2,0},{3,1},{4,6},{5,7},{6,4},{7,5},{8,10},{9,11},{10,... | collective-permute-start | bytes 1572872 | tf_op jit(solution)/shard_map/ppermute | solution.py:36
  116.0 25.5 %collective-permute-start.38 = (bf16[4,4,256,256]{3,2,1,0:T(8,128)(2,1)S(1)}, bf16[4,4,256,256]{3,2,1,0:T(8,128)(2,1)S(1)}, u32[]{:S(2)}, u32[]{:S(2)}) collective-permute-start(bf16[4,4,256,256]{3,2,1,0:T(8,128)(2,1)S(1)} %pad_maximum_fusion.refs_8_), channel_id=1, source_target_pairs={{0,32},{32,0},{1,33},{33,1},{2,34},{34,2},{3,35},{35,3},{4,36},{36... | collective-permute-start | bytes 6291464 | tf_op jit(solution)/shard_map/ppermute | solution.py:36
  116.1 6.0 %collective-permute-start.29 = (bf16[256,256]{1,0:T(8,128)(2,1)S(1)}, bf16[256,256]{1,0:T(8,128)(2,1)S(1)}, u32[]{:S(2)}, u32[]{:S(2)}) collective-permute-start(bf16[256,256]{1,0:T(8,128)(2,1)S(1)} %bitcast.53), channel_id=1, source_target_pairs={{0,28},{4,0},{8,4},{12,8},{16,12},{20,16},{24,20},{28,24},{1,29},{... | collective-permute-start | bytes 393224 | tf_op jit(solution)/shard_map/ppermute | solution.py:36
  117.7 9.5 %collective-permute-start.30 = (bf16[256,256]{1,0:T(8,128)(2,1)S(1)}, bf16[256,256]{1,0:T(8,128)(2,1)S(1)}, u32[]{:S(2)}, u32[]{:S(2)}) collective-permute-start(bf16[256,256]{1,0:T(8,128)(2,1)S(1)} %bitcast.54), channel_id=1, source_target_pairs={{0,4},{4,8},{8,12},{12,16},{16,20},{20,24},{24,28},{28,0},{1,5},{5... | collective-permute-start | bytes 393224 | tf_op jit(solution)/shard_map/ppermute | solution.py:36
  118.2 9.0 %collective-permute-start.31 = (bf16[256,256]{1,0:T(8,128)(2,1)S(1)}, bf16[256,256]{1,0:T(8,128)(2,1)S(1)}, u32[]{:S(2)}, u32[]{:S(2)}) collective-permute-start(bf16[256,256]{1,0:T(8,128)(2,1)S(1)} %bitcast.55), channel_id=1, source_target_pairs={{0,24},{4,28},{8,0},{12,4},{16,8},{20,12},{24,16},{28,20},{1,25},{... | collective-permute-start | bytes 393224 | tf_op jit(solution)/shard_map/ppermute | solution.py:36
  119.7 9.9 %collective-permute-start.32 = (bf16[256,256]{1,0:T(8,128)(2,1)S(1)}, bf16[256,256]{1,0:T(8,128)(2,1)S(1)}, u32[]{:S(2)}, u32[]{:S(2)}) collective-permute-start(bf16[256,256]{1,0:T(8,128)(2,1)S(1)} %bitcast.56), channel_id=1, source_target_pairs={{0,8},{4,12},{8,16},{12,20},{16,24},{20,28},{24,0},{28,4},{1,9},{5... | collective-permute-start | bytes 393224 | tf_op jit(solution)/shard_map/ppermute | solution.py:36
  129.6 6.0 %collective-permute-start.35 = (bf16[128,256]{1,0:T(8,128)(2,1)S(1)}, bf16[128,256]{1,0:T(8,128)(2,1)S(1)}, u32[]{:S(2)}, u32[]{:S(2)}) collective-permute-start(bf16[128,256]{1,0:T(8,128)(2,1)S(1)} %slice.34), channel_id=1, source_target_pairs={{0,24},{4,28},{8,0},{12,4},{16,8},{20,12},{24,16},{28,20},{1,25},{... | collective-permute-start | bytes 196616 | tf_op jit(solution)/shard_map/ppermute | solution.py:36
  129.9 8.2 %collective-permute-start.36 = (bf16[128,256]{1,0:T(8,128)(2,1)S(1)}, bf16[128,256]{1,0:T(8,128)(2,1)S(1)}, u32[]{:S(2)}, u32[]{:S(2)}) collective-permute-start(bf16[128,256]{1,0:T(8,128)(2,1)S(1)} %slice.35), channel_id=1, source_target_pairs={{0,8},{4,12},{8,16},{12,20},{16,24},{20,28},{24,0},{28,4},{1,9},{5... | collective-permute-start | bytes 196616 | tf_op jit(solution)/shard_map/ppermute | solution.py:36
  132.6 5.7 %collective-permute-start.33 = (bf16[256,256]{1,0:T(8,128)(2,1)S(1)}, bf16[256,256]{1,0:T(8,128)(2,1)S(1)}, u32[]{:S(2)}, u32[]{:S(2)}) collective-permute-start(bf16[256,256]{1,0:T(8,128)(2,1)S(1)} %collective-permute-done.31.refs_2_), channel_id=1, source_target_pairs={{0,28},{4,0},{8,4},{12,8},{16,12},{20,16},{24,20},{28,24},{1,29},{... | collective-permute-start | bytes 393224 | tf_op jit(solution)/shard_map/ppermute | solution.py:36
  135.3 6.2 %collective-permute-start.34 = (bf16[256,256]{1,0:T(8,128)(2,1)S(1)}, bf16[256,256]{1,0:T(8,128)(2,1)S(1)}, u32[]{:S(2)}, u32[]{:S(2)}) collective-permute-start(bf16[256,256]{1,0:T(8,128)(2,1)S(1)} %collective-permute-done.32.refs_4_), channel_id=1, source_target_pairs={{0,4},{4,8},{8,12},{12,16},{16,20},{20,24},{24,28},{28,0},{1,5},{5... | collective-permute-start | bytes 393224 | tf_op jit(solution)/shard_map/ppermute | solution.py:36
  143.9 8.3 %collective-permute-start.39 = (bf16[256,256]{1,0:T(8,128)(2,1)S(1)}, bf16[256,256]{1,0:T(8,128)(2,1)S(1)}, u32[]{:S(2)}, u32[]{:S(2)}) collective-permute-start(bf16[256,256]{1,0:T(8,128)(2,1)S(1)} %get-tuple-element.97), channel_id=1, source_target_pairs={{0,1},{1,2},{2,3},{3,0},{4,5},{5,6},{6,7},{7,4},{8,9},{9,10},{10,1... | collective-permute-start | bytes 393224 | tf_op jit(solution)/shard_map/ppermute | solution.py:36
  148.3 6.5 %collective-permute-start.40 = (bf16[256,256]{1,0:T(8,128)(2,1)S(1)}, bf16[256,256]{1,0:T(8,128)(2,1)S(1)}, u32[]{:S(2)}, u32[]{:S(2)}) collective-permute-start(bf16[256,256]{1,0:T(8,128)(2,1)S(1)} %get-tuple-element.99), channel_id=1, source_target_pairs={{0,2},{1,3},{2,0},{3,1},{4,6},{5,7},{6,4},{7,5},{8,10},{9,11},{10,... | collective-permute-start | bytes 393224 | tf_op jit(solution)/shard_map/ppermute | solution.py:36
  149.4 6.8 %collective-permute-start.41 = (bf16[256,256]{1,0:T(8,128)(2,1)S(1)}, bf16[256,256]{1,0:T(8,128)(2,1)S(1)}, u32[]{:S(2)}, u32[]{:S(2)}) collective-permute-start(bf16[256,256]{1,0:T(8,128)(2,1)S(1)} %get-tuple-element.98), channel_id=1, source_target_pairs={{0,3},{1,0},{2,1},{3,2},{4,7},{5,4},{6,5},{7,6},{8,11},{9,8},{10,9... | collective-permute-start | bytes 393224 | tf_op jit(solution)/shard_map/ppermute | solution.py:36
  (9 other events, 81.4 us)
where the time goes:
time: 157 us
  starting transfers between devices  71.7 us (46%)
  waiting for transfers between devices  49 us (31%)
  Pallas kernels  17.9 us (11%)
  blocking collectives  9.86 us (6%)
  local copies, waits for them, and re-layouts  3.94 us (3%)
  other arithmetic  2.49 us (2%)
  matrix products  1.77 us (1%)
    ppermute x41, starting transfers between devices, shift(): return lax.ppermute(values, axis, [(i, (i + step) % n) for i in range(n)])  58.4 us
    ppermute x41, waiting for transfers between devices, shift(): return lax.ppermute(values, axis, [(i, (i + step) % n) for i in range(n)])  49 us
    all_to_all x1, starting transfers between devices, over_ctx(): return lax.all_to_all(values, CTX, split_axis=0, concat_axis=0, tiled=True)  11.8 us
    all_to_all x1, blocking collectives, over_ctx(): return lax.all_to_all(values, CTX, split_axis=0, concat_axis=0, tiled=True)  9.86 us
    pallas_call x2, Pallas kernels, slot(): pl.pallas_call(functools.partial(slot_kernel, blocks, len(names)), out_sh...  6.23 us
    pallas_call x1, Pallas kernels, filtered(): pl.pallas_call(filter_kernel, out_shape=jax.ShapeDtypeStruct((8, 32, 256)...  3.74 us
    pallas_call x1, Pallas kernels, turned_weight(): pl.pallas_call(turn_kernel, out_shape=jax.ShapeDtypeStruct((2, 768, 1024)...  3.53 us
  transfers between devices with their start and end apart: 43, of which 26 were waited for; matrix products, arithmetic and copies ran while one was open for 4% of the time, Pallas kernels for 8%

commit v1 on v0

--- a/solution.py
+++ b/solution.py
@@ -338,10 +338,14 @@
     )(where, *[half for name in names for half in units[name]], weight)
 
 
-def sum_over_x(parts):
-    total = parts[0]
-    for k in (1, 2, 3):
-        total = total + shift(parts[k], "x", k).astype(jnp.float32)
+def moved_over_x(parts):
+    return [shift(parts[k], "x", k) for k in (1, 2, 3)]
+
+
+def sum_over_x(own, moved):
+    total = own
+    for part in moved:
+        total = total + part.astype(jnp.float32)
     return total[:96], shift(total[96:], "core", 1)
 
 
@@ -430,10 +434,10 @@
         [[("up1", 1), ("up2", 0)], [("down1", 1), ("down2", 0)]],
     )
     parts, rows[3], last = together(parts, rows[3], down[1])
-    pieces = [sum_over_x(parts)]
+    early, _ = together(parts, [up[1], down[0]])
+    moved = moved_over_x(early)
 
     units["across"] = [shift(up[0], "z", 1), shift(last, "z", -1)]
-    pieces[0], units["across"] = together(pieces[0], units["across"])
     parts = slot(
         where, units, weight,
         [[("down2", 0), ("down3", 1)], [("up2", 0), ("up3", 1)]],
@@ -441,7 +445,8 @@
     )
     rows[2], _ = together(rows[2], parts[0])
     rows[2] = shift(rows[2], "y", -2)
-    pieces.append(sum_over_x(parts))
+    parts, moved = together(parts, moved)
+    pieces = [sum_over_x(early[0], moved), sum_over_x(parts[0], moved_over_x(parts))]
     pieces = [piece[0] for piece in pieces] + [piece[1] for piece in pieces]
 
     gated = filtered(where, pieces, spectrum, skip)

time: 157 us -> 156 us (level)
  waiting for transfers between devices: 49 us -> 44.2 us
  starting transfers between devices: 71.7 us -> 74.7 us
    ppermute x41, waiting for transfers between devices: 49 us -> 44.2 us  [shift(): return lax.ppermute(values, axis, [(i, (i + step) % n) for i in range(n)])]
    ppermute x41, starting transfers between devices: 58.4 us -> 61.4 us  [shift(): return lax.ppermute(values, axis, [(i, (i + step) % n) for i in range(n)])]
  transfers between devices with their start and end apart: 43 -> 43, of which waited for: 26 -> 20; matrix products, arithmetic and copies ran while one was open for 4% -> 4% of each run, Pallas kernels for 8% -> 10%
where the time goes in v1:
time: 156 us; the launch traced here: 155 us
  starting transfers between devices  74.7 us (48%)
  waiting for transfers between devices  44.2 us (28%)
  Pallas kernels  17.9 us (11%)
  blocking collectives  10.1 us (6%)
  local copies, waits for them, and re-layouts  3.94 us (3%)
  other arithmetic  2.48 us (2%)
  matrix products  1.77 us (1%)
    ppermute x41, starting transfers between devices, shift(): return lax.ppermute(values, axis, [(i, (i + step) % n) for i in range(n)])  61.4 us
    ppermute x41, waiting for transfers between devices, shift(): return lax.ppermute(values, axis, [(i, (i + step) % n) for i in range(n)])  44.2 us
    all_to_all x1, starting transfers between devices, over_ctx(): return lax.all_to_all(values, CTX, split_axis=0, concat_axis=0, tiled=True)  11.8 us
    all_to_all x1, blocking collectives, over_ctx(): return lax.all_to_all(values, CTX, split_axis=0, concat_axis=0, tiled=True)  10.1 us
    pallas_call x2, Pallas kernels, slot(): pl.pallas_call(functools.partial(slot_kernel, blocks, len(names)), out_sh...  6.24 us
    pallas_call x1, Pallas kernels, filtered(): pl.pallas_call(filter_kernel, out_shape=jax.ShapeDtypeStruct((8, 32, 256)...  3.73 us
    pallas_call x1, Pallas kernels, turned_weight(): pl.pallas_call(turn_kernel, out_shape=jax.ShapeDtypeStruct((2, 768, 1024)...  3.53 us
  transfers between devices with their start and end apart: 43, of which 20 were waited for; matrix products, arithmetic and copies ran while one was open for 4% of the time, Pallas kernels for 10%

profile of v1, /device:TPU:24, one launch (start us, length us, event | category | flops | bytes accessed | tf_op | source)
XLA Modules:
  0.0 155.3 jit_solution(11713814295144823036)
XLA Ops:
  0.0 1.6 %collective-permute-start = (bf16[256,256]{1,0:T(8,128)(2,1)}, bf16[256,256]{1,0:T(8,128)(2,1)S(1)}, u32[]{:S(2)}, u32[]{:S(2)}) collective-permute-start(bf16[256,256]{1,0:T(8,128)(2,1)} %param.10), channel_id=1, source_target_pairs={{0,0},{1,1},{2,2},{3,3},{4,4},{5,5},{6,6},{7,7},{8,64},{9,65},{10,... | collective-permute-start | bytes 393224 | tf_op jit(solution)/shard_map/ppermute | solution.py:395
  1.6 1.8 %convolution_convert_fusion = bf16[2,256,2,256]{1,3,2,0:T(8,128)(2,1)S(1)} fusion(bf16[256,256]{1,0:T(8,128)(2,1)} %constant.203, bf16[256,256]{1,0:T(8,128)(2,1)} %constant.204, pred[2]{0:T(512)(128)(4,1)S(1)} %add_compare_fusion, f32[2,2,256,256]{3,2,1,0:T(8,128)} %param.12), kind=kOutput, calls=%fused_computation.1 | convolution fusion | flops 134873088 | bytes 1835010 | tf_op jit(solution)/shard_map/plgc,lgh->plch/dot_general | solution.py:187
  4.2 11.8 %all-to-all-start = ((bf16[8,2,2,32,256]{4,3,2,1,0:T(8,128)(2,1)}), bf16[8,2,2,32,256]{4,3,2,1,0:T(8,128)(2,1)S(1)}, u32[]{:S(2)}, u32[]{:S(2)}) async-start(bf16[8,2,2,32,256]{4,3,2,1,0:T(8,128)(2,1)} %bitcast.52), calls=%async_computation | async-start | bytes 1048576 | tf_op jit(solution)/shard_map/all_to_all | solution.py:387
  17.8 2.2 %collective-permute-start.3 = (bf16[256,256]{1,0:T(8,128)(2,1)S(1)}, bf16[256,256]{1,0:T(8,128)(2,1)}, u32[]{:S(2)}, u32[]{:S(2)}) collective-permute-start(bf16[256,256]{1,0:T(8,128)(2,1)S(1)} %collective-permute-done.refs_0_), channel_id=1, source_target_pairs={{0,1},{1,2},{2,3},{3,0},{4,5},{5,6},{6,7},{7,4},{8,9},{9,10},{10,1... | collective-permute-start | bytes 393224 | tf_op jit(solution)/shard_map/ppermute | solution.py:36
  20.0 2.7 %dynamic-slice_bitcast_fusion = (bf16[4,256,256]{2,1,0:T(8,128)(2,1)}, bf16[4,256,256]{2,1,0:T(8,128)(2,1)S(1)}, bf16[4,256,256]{2,1,0:T(8,128)(2,1)}, bf16[4,256,256]{2,1,0:T(8,128)(2,1)S(1)}) fusion(bf16[2,4,4,256,256]{4,3,2,1,0:T(8,128)(2,1)} %bitcast.61, s32[]{:T(128)S(6)} %select_n.56, s32[]{:T(128)S(6)} %select_n.68, s32[]{:T(128)S(6)} %select_n.65, ...), kind=kLoop, calls=%fused_computation.4 | loop fusion | bytes 4194324 | tf_op jit(solution)/shard_map/jit(dynamic_index_in_dim)/squeeze | solution.py:407
  22.7 3.4 %collective-permute-done.1.refs_1_ = bf16[256,256]{1,0:T(8,128)(2,1)S(1)} collective-permute-done((bf16[256,256]{1,0:T(8,128)(2,1)S(1)}, bf16[256,256]{1,0:T(8,128)(2,1)S(1)}, u32[]{:S(2)}, u32[]{:S(2)}) %collective-permute-start.1) | collective-permute-done | bytes 131104 | tf_op jit(solution)/shard_map/ppermute | solution.py:36
  26.8 1.9 %shard_map.100 = (bf16[128,1024]{1,0:T(8,128)(2,1)}, bf16[128,1024]{1,0:T(8,128)(2,1)}) custom-call(bf16[256,256]{1,0:T(8,128)(2,1)} %copy-done.11, bf16[256,256]{1,0:T(8,128)(2,1)} %copy-done.12, bf16[256,256]{1,0:T(8,128)(2,1)} %copy-done.13, bf16[256,256]{1,0:T(8,128)(2,1)} %collective-permute-done.3.refs_3_), custom_call_target="tpu_custom_call" | custom-call | flops 2000000000 | bytes 6000000 | tf_op jit(solution)/shard_map/pallas_call | solution.py:272
  29.8 2.2 %collective-permute-start.5 = (bf16[128,1024]{1,0:T(8,128)(2,1)}, bf16[128,1024]{1,0:T(8,128)(2,1)S(1)}, u32[]{:S(2)}, u32[]{:S(2)}) collective-permute-start(bf16[128,1024]{1,0:T(8,128)(2,1)} %get-tuple-element.60.refs_5_), channel_id=1, source_target_pairs={{0,28},{4,0},{8,4},{12,8},{16,12},{20,16},{24,20},{28,24},{1,29},{... | collective-permute-start | bytes 786440 | tf_op jit(solution)/shard_map/ppermute | solution.py:36
  32.0 4.9 %collective-permute-start.4 = (bf16[128,1024]{1,0:T(8,128)(2,1)}, bf16[128,1024]{1,0:T(8,128)(2,1)S(1)}, u32[]{:S(2)}, u32[]{:S(2)}) collective-permute-start(bf16[128,1024]{1,0:T(8,128)(2,1)} %get-tuple-element.59.refs_4_), channel_id=1, source_target_pairs={{0,28},{4,0},{8,4},{12,8},{16,12},{20,16},{24,20},{28,24},{1,29},{... | collective-permute-start | bytes 786440 | tf_op jit(solution)/shard_map/ppermute | solution.py:36
  36.9 2.4 %collective-permute-done.10.refs_6_ = bf16[128,1024]{1,0:T(8,128)(2,1)S(1)} collective-permute-done((bf16[128,1024]{1,0:T(8,128)(2,1)}, bf16[128,1024]{1,0:T(8,128)(2,1)S(1)}, u32[]{:S(2)}, u32[]{:S(2)}) %collective-permute-start.10) | collective-permute-done | bytes 262176 | tf_op jit(solution)/shard_map/ppermute | solution.py:36
  40.0 3.5 %shard_map.101.refs_10_ = bf16[2,768,1024]{2,1,0:T(8,128)(2,1)S(1)} custom-call(s32[4]{0:T(128)S(1)} %pad_add_fusion.place_ref, bf16[3,4,256,256]{3,2,1,0:T(8,128)(2,1)S(1)} %bitcast.58, bf16[3,4,256,256]{3,2,1,0:T(8,128)(2,1)} %bitcast.16.sibling_ref), custom_call_target="tpu_custom_call" | custom-call | flops 3000000000 | bytes 9000000 | tf_op jit(solution)/shard_map/pallas_call | solution.py:238
  43.5 1.4 collective-permute-done.8.refs_7_
  45.0 4.9 %collective-permute-start.9 = (bf16[128,1024]{1,0:T(8,128)(2,1)S(1)}, bf16[128,1024]{1,0:T(8,128)(2,1)S(1)}, u32[]{:S(2)}, u32[]{:S(2)}) collective-permute-start(bf16[128,1024]{1,0:T(8,128)(2,1)S(1)} %collective-permute-done.5.refs_1_), channel_id=1, source_target_pairs={{0,28},{4,0},{8,4},{12,8},{16,12},{20,16},{24,20},{28,24},{1,29},{... | collective-permute-start | bytes 786440 | tf_op jit(solution)/shard_map/ppermute | solution.py:36
  49.9 2.0 %collective-permute-start.6 = (bf16[128,1024]{1,0:T(8,128)(2,1)S(1)}, bf16[128,1024]{1,0:T(8,128)(2,1)S(1)}, u32[]{:S(2)}, u32[]{:S(2)}) collective-permute-start(bf16[128,1024]{1,0:T(8,128)(2,1)S(1)} %collective-permute-done.4.refs_0_), channel_id=1, source_target_pairs={{0,28},{4,0},{8,4},{12,8},{16,12},{20,16},{24,20},{28,24},{1,29},{... | collective-permute-start | bytes 786440 | tf_op jit(solution)/shard_map/ppermute | solution.py:36
  52.4 4.5 %collective-permute-done.12.refs_9_.refs_7_ = bf16[128,1024]{1,0:T(8,128)(2,1)S(1)} collective-permute-done((bf16[128,1024]{1,0:T(8,128)(2,1)S(1)}, bf16[128,1024]{1,0:T(8,128)(2,1)S(1)}, u32[]{:S(2)}, u32[]{:S(2)}) %collective-permute-start.12) | collective-permute-done | bytes 262176 | tf_op jit(solution)/shard_map/ppermute | solution.py:36
  57.0 2.2 %collective-permute-start.14 = (bf16[4,256,256]{2,1,0:T(8,128)(2,1)S(1)}, bf16[4,256,256]{2,1,0:T(8,128)(2,1)S(1)}, u32[]{:S(2)}, u32[]{:S(2)}) collective-permute-start(bf16[4,256,256]{2,1,0:T(8,128)(2,1)S(1)} %copy-done.10), channel_id=1, source_target_pairs={{0,1},{1,2},{2,3},{3,0},{4,5},{5,6},{6,7},{7,4},{8,9},{9,10},{10,1... | collective-permute-start | bytes 1572872 | tf_op jit(solution)/shard_map/ppermute | solution.py:36
  59.1 4.6 %collective-permute-start.17 = (bf16[128,1024]{1,0:T(8,128)(2,1)S(1)}, bf16[128,1024]{1,0:T(8,128)(2,1)S(1)}, u32[]{:S(2)}, u32[]{:S(2)}) collective-permute-start(bf16[128,1024]{1,0:T(8,128)(2,1)S(1)} %collective-permute-done.6.refs_2_), channel_id=1, source_target_pairs={{0,28},{4,0},{8,4},{12,8},{16,12},{20,16},{24,20},{28,24},{1,29},{... | collective-permute-start | bytes 786440 | tf_op jit(solution)/shard_map/ppermute | solution.py:36
  63.7 3.2 %collective-permute-start.15 = (bf16[128,1024]{1,0:T(8,128)(2,1)S(1)}, bf16[128,1024]{1,0:T(8,128)(2,1)S(1)}, u32[]{:S(2)}, u32[]{:S(2)}) collective-permute-start(bf16[128,1024]{1,0:T(8,128)(2,1)S(1)} %collective-permute-done.9.refs_3_), channel_id=1, source_target_pairs={{0,28},{4,0},{8,4},{12,8},{16,12},{20,16},{24,20},{28,24},{1,29},{... | collective-permute-start | bytes 786440 | tf_op jit(solution)/shard_map/ppermute | solution.py:36
  67.0 3.1 %shard_map.102 = (f32[192,512]{1,0:T(8,128)S(1)}, bf16[192,512]{1,0:T(8,128)(2,1)S(1)}, bf16[192,512]{1,0:T(8,128)(2,1)S(1)}, bf16[192,512]{1,0:T(8,128)(2,1)S(1)}) custom-call(s32[4]{0:T(128)S(1)} %pad_add_fusion.place_ref, bf16[128,1024]{1,0:T(8,128)(2,1)S(1)} %collective-permute-done.4.refs_0_, bf16[128,1024]{1,0:T(8,128)(2,1)S(1)} %collective-permute-done.5.refs_1_, ...), custom_call_target="tpu_custom_call" | custom-call | flops 3000000000 | bytes 9000000 | tf_op jit(solution)/shard_map/pallas_call | solution.py:323
  70.1 2.2 %collective-permute-done.15.refs_5_ = bf16[128,1024]{1,0:T(8,128)(2,1)S(1)} collective-permute-done((bf16[128,1024]{1,0:T(8,128)(2,1)S(1)}, bf16[128,1024]{1,0:T(8,128)(2,1)S(1)}, u32[]{:S(2)}, u32[]{:S(2)}) %collective-permute-start.15) | collective-permute-done | bytes 262176 | tf_op jit(solution)/shard_map/ppermute | solution.py:36
  72.3 3.7 %collective-permute-start.20 = (bf16[128,1024]{1,0:T(8,128)(2,1)S(1)}, bf16[128,1024]{1,0:T(8,128)(2,1)S(1)}, u32[]{:S(2)}, u32[]{:S(2)}) collective-permute-start(bf16[128,1024]{1,0:T(8,128)(2,1)S(1)} %collective-permute-done.15.refs_5_), channel_id=1, source_target_pairs={{0,28},{4,0},{8,4},{12,8},{16,12},{20,16},{24,20},{28,24},{1,29},{... | collective-permute-start | bytes 786440 | tf_op jit(solution)/shard_map/ppermute | solution.py:36
  76.0 2.0 %collective-permute-start.22 = (bf16[192,512]{1,0:T(8,128)(2,1)S(1)}, bf16[192,512]{1,0:T(8,128)(2,1)S(1)}, u32[]{:S(2)}, u32[]{:S(2)}) collective-permute-start(bf16[192,512]{1,0:T(8,128)(2,1)S(1)} %get-tuple-element.84), channel_id=1, source_target_pairs={{0,128},{64,192},{128,0},{192,64},{1,129},{65,193},{129,1},{193,65... | collective-permute-start | bytes 589832 | tf_op jit(solution)/shard_map/ppermute | solution.py:36
  78.0 2.5 %collective-permute-start.23 = (bf16[192,512]{1,0:T(8,128)(2,1)S(1)}, bf16[192,512]{1,0:T(8,128)(2,1)S(1)}, u32[]{:S(2)}, u32[]{:S(2)}) collective-permute-start(bf16[192,512]{1,0:T(8,128)(2,1)S(1)} %get-tuple-element.85), channel_id=1, source_target_pairs={{0,192},{64,0},{128,64},{192,128},{1,193},{65,1},{129,65},{193,129... | collective-permute-start | bytes 589832 | tf_op jit(solution)/shard_map/ppermute | solution.py:36
  80.5 3.1 %shard_map.103 = (f32[192,512]{1,0:T(8,128)S(1)}, bf16[192,512]{1,0:T(8,128)(2,1)S(1)}, bf16[192,512]{1,0:T(8,128)(2,1)S(1)}, bf16[192,512]{1,0:T(8,128)(2,1)S(1)}) custom-call(s32[4]{0:T(128)S(1)} %pad_add_fusion.place_ref, bf16[128,1024]{1,0:T(8,128)(2,1)S(1)} %collective-permute-done.19.refs_0_, bf16[128,1024]{1,0:T(8,128)(2,1)S(1)} %collective-permute-done.20.refs_1_, ...), custom_call_target="tpu_custom_call" | custom-call | flops 3000000000 | bytes 9000000 | tf_op jit(solution)/shard_map/pallas_call | solution.py:323
  83.6 2.0 %collective-permute-done.21 = bf16[192,512]{1,0:T(8,128)(2,1)S(1)} collective-permute-done((bf16[192,512]{1,0:T(8,128)(2,1)S(1)}, bf16[192,512]{1,0:T(8,128)(2,1)S(1)}, u32[]{:S(2)}, u32[]{:S(2)}) %collective-permute-start.21) | collective-permute-done | bytes 196640 | tf_op jit(solution)/shard_map/ppermute | solution.py:36
  86.8 2.8 %collective-permute-start.24 = (bf16[192,512]{1,0:T(8,128)(2,1)S(1)}, bf16[192,512]{1,0:T(8,128)(2,1)S(1)}, u32[]{:S(2)}, u32[]{:S(2)}) collective-permute-start(bf16[192,512]{1,0:T(8,128)(2,1)S(1)} %get-tuple-element.90), channel_id=1, source_target_pairs={{0,64},{64,128},{128,192},{192,0},{1,65},{65,129},{129,193},{193,1... | collective-permute-start | bytes 589832 | tf_op jit(solution)/shard_map/ppermute | solution.py:36
  89.6 1.4 collective-permute-start.25
  91.0 1.4 collective-permute-start.26
  93.7 3.1 %collective-permute-done.25 = bf16[192,512]{1,0:T(8,128)(2,1)S(1)} collective-permute-done((bf16[192,512]{1,0:T(8,128)(2,1)S(1)}, bf16[192,512]{1,0:T(8,128)(2,1)S(1)}, u32[]{:S(2)}, u32[]{:S(2)}) %collective-permute-start.25) | collective-permute-done | bytes 196640 | tf_op jit(solution)/shard_map/ppermute | solution.py:36
  97.1 2.4 %collective-permute-start.37 = (bf16[4,256,256]{2,1,0:T(8,128)(2,1)S(1)}, bf16[4,256,256]{2,1,0:T(8,128)(2,1)}, u32[]{:S(2)}, u32[]{:S(2)}) collective-permute-start(bf16[4,256,256]{2,1,0:T(8,128)(2,1)S(1)} %get-tuple-element.101), channel_id=1, source_target_pairs={{0,2},{1,3},{2,0},{3,1},{4,6},{5,7},{6,4},{7,5},{8,10},{9,11},{10,... | collective-permute-start | bytes 1572872 | tf_op jit(solution)/shard_map/ppermute | solution.py:36
  99.6 3.7 %shard_map.104 = bf16[8,32,256]{2,1,0:T(8,128)(2,1)S(1)} custom-call(s32[4]{0:T(128)S(1)} %pad_add_fusion.place_ref, f32[32,1]{1,0:T(8,128)S(1)} %copy.25.refs_0_, f32[96,512]{1,0:T(8,128)S(1)} %get-tuple-element.117.refs_1_, f32[96,512]{1,0:T(8,128)S(1)} %get-tuple-element.115.refs_2_, f32[96,512]{1,0:T(8,128)S(1)} %collective-permute-done.27.refs_3_, ...), custom_call_target="tpu_custom_call" | custom-call | flops 3000000000 | bytes 9000000 | tf_op jit(solution)/shard_map/pallas_call | solution.py:158
  103.4 10.1 %all_to_all.10 = bf16[8,32,256]{2,1,0:T(8,128)(2,1)S(1)} all-to-all(bf16[8,32,256]{2,1,0:T(8,128)(2,1)S(1)} %shard_map.104), channel_id=1, replica_groups=mesh['x'=4,'core'=2,'z'=8,'y'=4] {'x','core'}, dimensions={0} | all-to-all | bytes 262144 | tf_op jit(solution)/shard_map/all_to_all | solution.py:387
  113.5 1.5 pad_maximum_fusion.refs_8_
  115.2 2.0 %collective-permute-start.30 = (bf16[256,256]{1,0:T(8,128)(2,1)S(1)}, bf16[256,256]{1,0:T(8,128)(2,1)S(1)}, u32[]{:S(2)}, u32[]{:S(2)}) collective-permute-start(bf16[256,256]{1,0:T(8,128)(2,1)S(1)} %bitcast.54), channel_id=1, source_target_pairs={{0,4},{4,8},{8,12},{12,16},{16,20},{20,24},{24,28},{28,0},{1,5},{5... | collective-permute-start | bytes 393224 | tf_op jit(solution)/shard_map/ppermute | solution.py:36
  117.2 4.3 %collective-permute-start.31 = (bf16[256,256]{1,0:T(8,128)(2,1)S(1)}, bf16[256,256]{1,0:T(8,128)(2,1)S(1)}, u32[]{:S(2)}, u32[]{:S(2)}) collective-permute-start(bf16[256,256]{1,0:T(8,128)(2,1)S(1)} %bitcast.55), channel_id=1, source_target_pairs={{0,24},{4,28},{8,0},{12,4},{16,8},{20,12},{24,16},{28,20},{1,25},{... | collective-permute-start | bytes 393224 | tf_op jit(solution)/shard_map/ppermute | solution.py:36
  121.5 2.4 %collective-permute-done.29.refs_1_ = bf16[256,256]{1,0:T(8,128)(2,1)S(1)} collective-permute-done((bf16[256,256]{1,0:T(8,128)(2,1)S(1)}, bf16[256,256]{1,0:T(8,128)(2,1)S(1)}, u32[]{:S(2)}, u32[]{:S(2)}) %collective-permute-start.29) | collective-permute-done | bytes 131104 | tf_op jit(solution)/shard_map/ppermute | solution.py:36
  123.9 3.5 %collective-permute-done.31.refs_2_ = bf16[256,256]{1,0:T(8,128)(2,1)S(1)} collective-permute-done((bf16[256,256]{1,0:T(8,128)(2,1)S(1)}, bf16[256,256]{1,0:T(8,128)(2,1)S(1)}, u32[]{:S(2)}, u32[]{:S(2)}) %collective-permute-start.31) | collective-permute-done | bytes 131104 | tf_op jit(solution)/shard_map/ppermute | solution.py:36
  127.4 4.3 %collective-permute-done.32.refs_4_ = bf16[256,256]{1,0:T(8,128)(2,1)S(1)} collective-permute-done((bf16[256,256]{1,0:T(8,128)(2,1)S(1)}, bf16[256,256]{1,0:T(8,128)(2,1)S(1)}, u32[]{:S(2)}, u32[]{:S(2)}) %collective-permute-start.32) | collective-permute-done | bytes 131104 | tf_op jit(solution)/shard_map/ppermute | solution.py:36
  131.6 2.2 %collective-permute-start.35 = (bf16[128,256]{1,0:T(8,128)(2,1)S(1)}, bf16[128,256]{1,0:T(8,128)(2,1)S(1)}, u32[]{:S(2)}, u32[]{:S(2)}) collective-permute-start(bf16[128,256]{1,0:T(8,128)(2,1)S(1)} %slice.34), channel_id=1, source_target_pairs={{0,24},{4,28},{8,0},{12,4},{16,8},{20,12},{24,16},{28,20},{1,25},{... | collective-permute-start | bytes 196616 | tf_op jit(solution)/shard_map/ppermute | solution.py:36
  134.6 2.4 %collective-permute-start.33 = (bf16[256,256]{1,0:T(8,128)(2,1)S(1)}, bf16[256,256]{1,0:T(8,128)(2,1)S(1)}, u32[]{:S(2)}, u32[]{:S(2)}) collective-permute-start(bf16[256,256]{1,0:T(8,128)(2,1)S(1)} %collective-permute-done.31.refs_2_), channel_id=1, source_target_pairs={{0,28},{4,0},{8,4},{12,8},{16,12},{20,16},{24,20},{28,24},{1,29},{... | collective-permute-start | bytes 393224 | tf_op jit(solution)/shard_map/ppermute | solution.py:36
  137.6 2.9 %collective-permute-done.36 = bf16[128,256]{1,0:T(8,128)(2,1)S(1)} collective-permute-done((bf16[128,256]{1,0:T(8,128)(2,1)S(1)}, bf16[128,256]{1,0:T(8,128)(2,1)S(1)}, u32[]{:S(2)}, u32[]{:S(2)}) %collective-permute-start.36) | collective-permute-done | bytes 65568 | tf_op jit(solution)/shard_map/ppermute | solution.py:36
  140.5 2.6 %collective-permute-done.34.refs_6_ = bf16[256,256]{1,0:T(8,128)(2,1)S(1)} collective-permute-done((bf16[256,256]{1,0:T(8,128)(2,1)S(1)}, bf16[256,256]{1,0:T(8,128)(2,1)S(1)}, u32[]{:S(2)}, u32[]{:S(2)}) %collective-permute-start.34) | collective-permute-done | bytes 131104 | tf_op jit(solution)/shard_map/ppermute | solution.py:36
  143.2 2.4 %shard_map.105 = bf16[4,256,256]{2,1,0:T(8,128)(2,1)S(1)} custom-call(s32[4]{0:T(128)S(1)} %pad_add_fusion.place_ref, bf16[256,256]{1,0:T(8,128)(2,1)S(1)} %bitcast.57, bf16[256,256]{1,0:T(8,128)(2,1)S(1)} %collective-permute-done.29.refs_1_, bf16[256,256]{1,0:T(8,128)(2,1)S(1)} %collective-permute-done.31.refs_2_, ...), custom_call_target="tpu_custom_call" | custom-call | flops 2000000000 | bytes 6000000 | tf_op jit(solution)/shard_map/pallas_call | solution.py:375
  146.7 1.2 collective-permute-start.40
  147.9 1.3 collective-permute-start.41
  149.2 1.4 collective-permute-done.39
  150.7 2.6 %collective-permute-done.40 = bf16[256,256]{1,0:T(8,128)(2,1)S(1)} collective-permute-done((bf16[256,256]{1,0:T(8,128)(2,1)S(1)}, bf16[256,256]{1,0:T(8,128)(2,1)S(1)}, u32[]{:S(2)}, u32[]{:S(2)}) %collective-permute-start.40) | collective-permute-done | bytes 131104 | tf_op jit(solution)/shard_map/ppermute | solution.py:36
  153.3 1.3 collective-permute-done.41
  (91 shorter events, 11.9 us)
Async XLA Ops:
  0.0 99.4 %copy-start = (f32[256]{0:T(256)S(1)}, f32[256]{0:T(256)}, u32[]{:S(2)}) copy-start(f32[256]{0:T(256)} %param.13) | copy-start | bytes 3076
  0.0 39.9 %collective-permute-start.7 = (bf16[3,1024,256]{2,1,0:T(8,128)(2,1)}, bf16[3,1024,256]{2,1,0:T(8,128)(2,1)}, u32[]{:S(2)}, u32[]{:S(2)}) collective-permute-start(bf16[3,1024,256]{2,1,0:T(8,128)(2,1)} %param.11), channel_id=1, source_target_pairs={{0,32},{32,0},{1,33},{33,1},{2,34},{34,2},{3,35},{35,3},{4,36},{36... | collective-permute-start | bytes 4718600 | tf_op jit(solution)/shard_map/ppermute | solution.py:36
  0.0 16.0 %collective-permute-start = (bf16[256,256]{1,0:T(8,128)(2,1)}, bf16[256,256]{1,0:T(8,128)(2,1)S(1)}, u32[]{:S(2)}, u32[]{:S(2)}) collective-permute-start(bf16[256,256]{1,0:T(8,128)(2,1)} %param.10), channel_id=1, source_target_pairs={{0,0},{1,1},{2,2},{3,3},{4,4},{5,5},{6,6},{7,7},{8,64},{9,65},{10,... | collective-permute-start | bytes 393224 | tf_op jit(solution)/shard_map/ppermute | solution.py:395
  4.2 24.5 %all-to-all-start = ((bf16[8,2,2,32,256]{4,3,2,1,0:T(8,128)(2,1)}), bf16[8,2,2,32,256]{4,3,2,1,0:T(8,128)(2,1)S(1)}, u32[]{:S(2)}, u32[]{:S(2)}) async-start(bf16[8,2,2,32,256]{4,3,2,1,0:T(8,128)(2,1)} %bitcast.52), calls=%async_computation | async-start | bytes 1048576 | tf_op jit(solution)/shard_map/all_to_all | solution.py:387
  16.0 10.0 %collective-permute-start.1 = (bf16[256,256]{1,0:T(8,128)(2,1)S(1)}, bf16[256,256]{1,0:T(8,128)(2,1)S(1)}, u32[]{:S(2)}, u32[]{:S(2)}) collective-permute-start(bf16[256,256]{1,0:T(8,128)(2,1)S(1)} %collective-permute-done.refs_0_), channel_id=1, source_target_pairs={{0,3},{1,0},{2,1},{3,2},{4,7},{5,4},{6,5},{7,6},{8,11},{9,8},{10,9... | collective-permute-start | bytes 393224 | tf_op jit(solution)/shard_map/ppermute | solution.py:36
  16.9 9.2 %collective-permute-start.2 = (bf16[256,256]{1,0:T(8,128)(2,1)S(1)}, bf16[256,256]{1,0:T(8,128)(2,1)S(1)}, u32[]{:S(2)}, u32[]{:S(2)}) collective-permute-start(bf16[256,256]{1,0:T(8,128)(2,1)S(1)} %collective-permute-done.refs_0_), channel_id=1, source_target_pairs={{0,2},{1,3},{2,0},{3,1},{4,6},{5,7},{6,4},{7,5},{8,10},{9,11},{10,... | collective-permute-start | bytes 393224 | tf_op jit(solution)/shard_map/ppermute | solution.py:36
  17.8 9.0 %collective-permute-start.3 = (bf16[256,256]{1,0:T(8,128)(2,1)S(1)}, bf16[256,256]{1,0:T(8,128)(2,1)}, u32[]{:S(2)}, u32[]{:S(2)}) collective-permute-start(bf16[256,256]{1,0:T(8,128)(2,1)S(1)} %collective-permute-done.refs_0_), channel_id=1, source_target_pairs={{0,1},{1,2},{2,3},{3,0},{4,5},{5,6},{6,7},{7,4},{8,9},{9,10},{10,1... | collective-permute-start | bytes 393224 | tf_op jit(solution)/shard_map/ppermute | solution.py:36
  22.7 17.3 %copy-start.1 = (bf16[3,1024,256]{2,1,0:T(8,128)(2,1)S(1)}, bf16[3,1024,256]{2,1,0:T(8,128)(2,1)}, u32[]{:S(2)}) copy-start(bf16[3,1024,256]{2,1,0:T(8,128)(2,1)} %param.11) | copy-start | bytes 4718596
  28.7 10.6 %collective-permute-start.10 = (bf16[128,1024]{1,0:T(8,128)(2,1)}, bf16[128,1024]{1,0:T(8,128)(2,1)S(1)}, u32[]{:S(2)}, u32[]{:S(2)}) collective-permute-start(bf16[128,1024]{1,0:T(8,128)(2,1)} %get-tuple-element.59.refs_4_), channel_id=1, source_target_pairs={{0,4},{4,8},{8,12},{12,16},{16,20},{20,24},{24,28},{28,0},{1,5},{5... | collective-permute-start | bytes 786440 | tf_op jit(solution)/shard_map/ppermute | solution.py:36
  29.8 13.7 %collective-permute-start.5 = (bf16[128,1024]{1,0:T(8,128)(2,1)}, bf16[128,1024]{1,0:T(8,128)(2,1)S(1)}, u32[]{:S(2)}, u32[]{:S(2)}) collective-permute-start(bf16[128,1024]{1,0:T(8,128)(2,1)} %get-tuple-element.60.refs_5_), channel_id=1, source_target_pairs={{0,28},{4,0},{8,4},{12,8},{16,12},{20,16},{24,20},{28,24},{1,29},{... | collective-permute-start | bytes 786440 | tf_op jit(solution)/shard_map/ppermute | solution.py:36
  32.0 12.9 %collective-permute-start.8 = (bf16[128,1024]{1,0:T(8,128)(2,1)}, bf16[128,1024]{1,0:T(8,128)(2,1)S(1)}, u32[]{:S(2)}, u32[]{:S(2)}) collective-permute-start(bf16[128,1024]{1,0:T(8,128)(2,1)} %get-tuple-element.60.refs_5_), channel_id=1, source_target_pairs={{0,4},{4,8},{8,12},{12,16},{16,20},{20,24},{24,28},{28,0},{1,5},{5... | collective-permute-start | bytes 786440 | tf_op jit(solution)/shard_map/ppermute | solution.py:36
  32.0 17.8 %collective-permute-start.4 = (bf16[128,1024]{1,0:T(8,128)(2,1)}, bf16[128,1024]{1,0:T(8,128)(2,1)S(1)}, u32[]{:S(2)}, u32[]{:S(2)}) collective-permute-start(bf16[128,1024]{1,0:T(8,128)(2,1)} %get-tuple-element.59.refs_4_), channel_id=1, source_target_pairs={{0,28},{4,0},{8,4},{12,8},{16,12},{20,16},{24,20},{28,24},{1,29},{... | collective-permute-start | bytes 786440 | tf_op jit(solution)/shard_map/ppermute | solution.py:36
  39.3 13.1 %collective-permute-start.13 = (bf16[4,256,256]{2,1,0:T(8,128)(2,1)}, bf16[4,256,256]{2,1,0:T(8,128)(2,1)S(1)}, u32[]{:S(2)}, u32[]{:S(2)}) collective-permute-start(bf16[4,256,256]{2,1,0:T(8,128)(2,1)} %get-tuple-element.68), channel_id=1, source_target_pairs={{0,3},{1,0},{2,1},{3,2},{4,7},{5,4},{6,5},{7,6},{8,11},{9,8},{10,9... | collective-permute-start | bytes 1572872 | tf_op jit(solution)/shard_map/ppermute | solution.py:36
  39.9 12.0 %collective-permute-start.11 = (bf16[128,1024]{1,0:T(8,128)(2,1)S(1)}, bf16[128,1024]{1,0:T(8,128)(2,1)S(1)}, u32[]{:S(2)}, u32[]{:S(2)}) collective-permute-start(bf16[128,1024]{1,0:T(8,128)(2,1)S(1)} %collective-permute-done.10.refs_6_), channel_id=1, source_target_pairs={{0,4},{4,8},{8,12},{12,16},{16,20},{20,24},{24,28},{28,0},{1,5},{5... | collective-permute-start | bytes 786440 | tf_op jit(solution)/shard_map/ppermute | solution.py:36
  39.9 27.0 %copy-start.2 = (bf16[128,1024]{1,0:T(8,128)(2,1)S(1)}, bf16[128,1024]{1,0:T(8,128)(2,1)}, u32[]{:S(2)}) copy-start(bf16[128,1024]{1,0:T(8,128)(2,1)} %get-tuple-element.59.refs_4_) | copy-start | bytes 786436
  39.9 27.0 %copy-start.3 = (bf16[128,1024]{1,0:T(8,128)(2,1)S(1)}, bf16[128,1024]{1,0:T(8,128)(2,1)}, u32[]{:S(2)}) copy-start(bf16[128,1024]{1,0:T(8,128)(2,1)} %get-tuple-element.60.refs_5_) | copy-start | bytes 786436
  45.0 12.0 %collective-permute-start.12 = (bf16[128,1024]{1,0:T(8,128)(2,1)S(1)}, bf16[128,1024]{1,0:T(8,128)(2,1)S(1)}, u32[]{:S(2)}, u32[]{:S(2)}) collective-permute-start(bf16[128,1024]{1,0:T(8,128)(2,1)S(1)} %collective-permute-done.8.refs_7_), channel_id=1, source_target_pairs={{0,4},{4,8},{8,12},{12,16},{16,20},{20,24},{24,28},{28,0},{1,5},{5... | collective-permute-start | bytes 786440 | tf_op jit(solution)/shard_map/ppermute | solution.py:36
  45.0 12.0 %collective-permute-start.9 = (bf16[128,1024]{1,0:T(8,128)(2,1)S(1)}, bf16[128,1024]{1,0:T(8,128)(2,1)S(1)}, u32[]{:S(2)}, u32[]{:S(2)}) collective-permute-start(bf16[128,1024]{1,0:T(8,128)(2,1)S(1)} %collective-permute-done.5.refs_1_), channel_id=1, source_target_pairs={{0,28},{4,0},{8,4},{12,8},{16,12},{20,16},{24,20},{28,24},{1,29},{... | collective-permute-start | bytes 786440 | tf_op jit(solution)/shard_map/ppermute | solution.py:36
  49.9 9.3 %collective-permute-start.6 = (bf16[128,1024]{1,0:T(8,128)(2,1)S(1)}, bf16[128,1024]{1,0:T(8,128)(2,1)S(1)}, u32[]{:S(2)}, u32[]{:S(2)}) collective-permute-start(bf16[128,1024]{1,0:T(8,128)(2,1)S(1)} %collective-permute-done.4.refs_0_), channel_id=1, source_target_pairs={{0,28},{4,0},{8,4},{12,8},{16,12},{20,16},{24,20},{28,24},{1,29},{... | collective-permute-start | bytes 786440 | tf_op jit(solution)/shard_map/ppermute | solution.py:36
  51.9 11.8 %collective-permute-start.18 = (bf16[128,1024]{1,0:T(8,128)(2,1)S(1)}, bf16[128,1024]{1,0:T(8,128)(2,1)S(1)}, u32[]{:S(2)}, u32[]{:S(2)}) collective-permute-start(bf16[128,1024]{1,0:T(8,128)(2,1)S(1)} %collective-permute-done.11.refs_8_.refs_6_), channel_id=1, source_target_pairs={{0,4},{4,8},{8,12},{12,16},{16,20},{20,24},{24,28},{28,0},{1,5},{5... | collective-permute-start | bytes 786440 | tf_op jit(solution)/shard_map/ppermute | solution.py:36
  52.4 17.7 %copy-start.7 = (bf16[4,256,256]{2,1,0:T(8,128)(2,1)}, bf16[4,256,256]{2,1,0:T(8,128)(2,1)S(1)}, u32[]{:S(2)}) copy-start(bf16[4,256,256]{2,1,0:T(8,128)(2,1)S(1)} %collective-permute-done.13) | copy-start | bytes 1572868
  57.0 15.4 %collective-permute-start.14 = (bf16[4,256,256]{2,1,0:T(8,128)(2,1)S(1)}, bf16[4,256,256]{2,1,0:T(8,128)(2,1)S(1)}, u32[]{:S(2)}, u32[]{:S(2)}) collective-permute-start(bf16[4,256,256]{2,1,0:T(8,128)(2,1)S(1)} %copy-done.10), channel_id=1, source_target_pairs={{0,1},{1,2},{2,3},{3,0},{4,5},{5,6},{6,7},{7,4},{8,9},{9,10},{10,1... | collective-permute-start | bytes 1572872 | tf_op jit(solution)/shard_map/ppermute | solution.py:36
  59.1 16.9 %collective-permute-start.17 = (bf16[128,1024]{1,0:T(8,128)(2,1)S(1)}, bf16[128,1024]{1,0:T(8,128)(2,1)S(1)}, u32[]{:S(2)}, u32[]{:S(2)}) collective-permute-start(bf16[128,1024]{1,0:T(8,128)(2,1)S(1)} %collective-permute-done.6.refs_2_), channel_id=1, source_target_pairs={{0,28},{4,0},{8,4},{12,8},{16,12},{20,16},{24,20},{28,24},{1,29},{... | collective-permute-start | bytes 786440 | tf_op jit(solution)/shard_map/ppermute | solution.py:36
  63.7 16.8 %collective-permute-start.19 = (bf16[128,1024]{1,0:T(8,128)(2,1)S(1)}, bf16[128,1024]{1,0:T(8,128)(2,1)S(1)}, u32[]{:S(2)}, u32[]{:S(2)}) collective-permute-start(bf16[128,1024]{1,0:T(8,128)(2,1)S(1)} %collective-permute-done.18.refs_8_), channel_id=1, source_target_pairs={{0,4},{4,8},{8,12},{12,16},{16,20},{20,24},{24,28},{28,0},{1,5},{5... | collective-permute-start | bytes 786440 | tf_op jit(solution)/shard_map/ppermute | solution.py:36
  63.7 8.6 %collective-permute-start.15 = (bf16[128,1024]{1,0:T(8,128)(2,1)S(1)}, bf16[128,1024]{1,0:T(8,128)(2,1)S(1)}, u32[]{:S(2)}, u32[]{:S(2)}) collective-permute-start(bf16[128,1024]{1,0:T(8,128)(2,1)S(1)} %collective-permute-done.9.refs_3_), channel_id=1, source_target_pairs={{0,28},{4,0},{8,4},{12,8},{16,12},{20,16},{24,20},{28,24},{1,29},{... | collective-permute-start | bytes 786440 | tf_op jit(solution)/shard_map/ppermute | solution.py:36
  67.0 9.1 %collective-permute-start.16 = (bf16[128,1024]{1,0:T(8,128)(2,1)S(1)}, bf16[128,1024]{1,0:T(8,128)(2,1)S(1)}, u32[]{:S(2)}, u32[]{:S(2)}) collective-permute-start(bf16[128,1024]{1,0:T(8,128)(2,1)S(1)} %collective-permute-done.12.refs_9_.refs_7_), channel_id=1, source_target_pairs={{0,4},{4,8},{8,12},{12,16},{16,20},{20,24},{24,28},{28,0},{1,5},{5... | collective-permute-start | bytes 786440 | tf_op jit(solution)/shard_map/ppermute | solution.py:36
  72.3 8.2 %collective-permute-start.20 = (bf16[128,1024]{1,0:T(8,128)(2,1)S(1)}, bf16[128,1024]{1,0:T(8,128)(2,1)S(1)}, u32[]{:S(2)}, u32[]{:S(2)}) collective-permute-start(bf16[128,1024]{1,0:T(8,128)(2,1)S(1)} %collective-permute-done.15.refs_5_), channel_id=1, source_target_pairs={{0,28},{4,0},{8,4},{12,8},{16,12},{20,16},{24,20},{28,24},{1,29},{... | collective-permute-start | bytes 786440 | tf_op jit(solution)/shard_map/ppermute | solution.py:36
  76.0 9.6 %collective-permute-start.21 = (bf16[192,512]{1,0:T(8,128)(2,1)S(1)}, bf16[192,512]{1,0:T(8,128)(2,1)S(1)}, u32[]{:S(2)}, u32[]{:S(2)}) collective-permute-start(bf16[192,512]{1,0:T(8,128)(2,1)S(1)} %get-tuple-element.83), channel_id=1, source_target_pairs={{0,64},{64,128},{128,192},{192,0},{1,65},{65,129},{129,193},{193,1... | collective-permute-start | bytes 589832 | tf_op jit(solution)/shard_map/ppermute | solution.py:36
  76.0 9.6 %collective-permute-start.22 = (bf16[192,512]{1,0:T(8,128)(2,1)S(1)}, bf16[192,512]{1,0:T(8,128)(2,1)S(1)}, u32[]{:S(2)}, u32[]{:S(2)}) collective-permute-start(bf16[192,512]{1,0:T(8,128)(2,1)S(1)} %get-tuple-element.84), channel_id=1, source_target_pairs={{0,128},{64,192},{128,0},{192,64},{1,129},{65,193},{129,1},{193,65... | collective-permute-start | bytes 589832 | tf_op jit(solution)/shard_map/ppermute | solution.py:36
  78.0 8.8 %collective-permute-start.23 = (bf16[192,512]{1,0:T(8,128)(2,1)S(1)}, bf16[192,512]{1,0:T(8,128)(2,1)S(1)}, u32[]{:S(2)}, u32[]{:S(2)}) collective-permute-start(bf16[192,512]{1,0:T(8,128)(2,1)S(1)} %get-tuple-element.85), channel_id=1, source_target_pairs={{0,192},{64,0},{128,64},{192,128},{1,193},{65,1},{129,65},{193,129... | collective-permute-start | bytes 589832 | tf_op jit(solution)/shard_map/ppermute | solution.py:36
  86.8 6.9 %collective-permute-start.24 = (bf16[192,512]{1,0:T(8,128)(2,1)S(1)}, bf16[192,512]{1,0:T(8,128)(2,1)S(1)}, u32[]{:S(2)}, u32[]{:S(2)}) collective-permute-start(bf16[192,512]{1,0:T(8,128)(2,1)S(1)} %get-tuple-element.90), channel_id=1, source_target_pairs={{0,64},{64,128},{128,192},{192,0},{1,65},{65,129},{129,193},{193,1... | collective-permute-start | bytes 589832 | tf_op jit(solution)/shard_map/ppermute | solution.py:36
  89.6 7.2 %collective-permute-start.25 = (bf16[192,512]{1,0:T(8,128)(2,1)S(1)}, bf16[192,512]{1,0:T(8,128)(2,1)S(1)}, u32[]{:S(2)}, u32[]{:S(2)}) collective-permute-start(bf16[192,512]{1,0:T(8,128)(2,1)S(1)} %get-tuple-element.91), channel_id=1, source_target_pairs={{0,128},{64,192},{128,0},{192,64},{1,129},{65,193},{129,1},{193,65... | collective-permute-start | bytes 589832 | tf_op jit(solution)/shard_map/ppermute | solution.py:36
  91.0 5.8 %collective-permute-start.26 = (bf16[192,512]{1,0:T(8,128)(2,1)S(1)}, bf16[192,512]{1,0:T(8,128)(2,1)S(1)}, u32[]{:S(2)}, u32[]{:S(2)}) collective-permute-start(bf16[192,512]{1,0:T(8,128)(2,1)S(1)} %get-tuple-element.92), channel_id=1, source_target_pairs={{0,192},{64,0},{128,64},{192,128},{1,193},{65,1},{129,65},{193,129... | collective-permute-start | bytes 589832 | tf_op jit(solution)/shard_map/ppermute | solution.py:36
  92.5 7.0 %collective-permute-start.27 = (f32[96,512]{1,0:T(8,128)S(1)}, f32[96,512]{1,0:T(8,128)S(1)}, u32[]{:S(2)}, u32[]{:S(2)}) collective-permute-start(f32[96,512]{1,0:T(8,128)S(1)} %get-tuple-element.116), channel_id=1, source_target_pairs={{0,32},{32,0},{1,33},{33,1},{2,34},{34,2},{3,35},{35,3},{4,36},{36... | collective-permute-start | bytes 589832 | tf_op jit(solution)/shard_map/ppermute | solution.py:36
  97.0 2.6 %collective-permute-start.28 = (f32[96,512]{1,0:T(8,128)S(1)}, f32[96,512]{1,0:T(8,128)S(1)}, u32[]{:S(2)}, u32[]{:S(2)}) collective-permute-start(f32[96,512]{1,0:T(8,128)S(1)} %get-tuple-element.114), channel_id=1, source_target_pairs={{0,32},{32,0},{1,33},{33,1},{2,34},{34,2},{3,35},{35,3},{4,36},{36... | collective-permute-start | bytes 589832 | tf_op jit(solution)/shard_map/ppermute | solution.py:36
  97.1 16.5 %collective-permute-start.37 = (bf16[4,256,256]{2,1,0:T(8,128)(2,1)S(1)}, bf16[4,256,256]{2,1,0:T(8,128)(2,1)}, u32[]{:S(2)}, u32[]{:S(2)}) collective-permute-start(bf16[4,256,256]{2,1,0:T(8,128)(2,1)S(1)} %get-tuple-element.101), channel_id=1, source_target_pairs={{0,2},{1,3},{2,0},{3,1},{4,6},{5,7},{6,4},{7,5},{8,10},{9,11},{10,... | collective-permute-start | bytes 1572872 | tf_op jit(solution)/shard_map/ppermute | solution.py:36
  115.0 28.1 %collective-permute-start.38 = (bf16[4,4,256,256]{3,2,1,0:T(8,128)(2,1)S(1)}, bf16[4,4,256,256]{3,2,1,0:T(8,128)(2,1)S(1)}, u32[]{:S(2)}, u32[]{:S(2)}) collective-permute-start(bf16[4,4,256,256]{3,2,1,0:T(8,128)(2,1)S(1)} %pad_maximum_fusion.refs_8_), channel_id=1, source_target_pairs={{0,32},{32,0},{1,33},{33,1},{2,34},{34,2},{3,35},{35,3},{4,36},{36... | collective-permute-start | bytes 6291464 | tf_op jit(solution)/shard_map/ppermute | solution.py:36
  115.1 8.7 %collective-permute-start.29 = (bf16[256,256]{1,0:T(8,128)(2,1)S(1)}, bf16[256,256]{1,0:T(8,128)(2,1)S(1)}, u32[]{:S(2)}, u32[]{:S(2)}) collective-permute-start(bf16[256,256]{1,0:T(8,128)(2,1)S(1)} %bitcast.53), channel_id=1, source_target_pairs={{0,28},{4,0},{8,4},{12,8},{16,12},{20,16},{24,20},{28,24},{1,29},{... | collective-permute-start | bytes 393224 | tf_op jit(solution)/shard_map/ppermute | solution.py:36
  115.2 8.6 %collective-permute-start.30 = (bf16[256,256]{1,0:T(8,128)(2,1)S(1)}, bf16[256,256]{1,0:T(8,128)(2,1)S(1)}, u32[]{:S(2)}, u32[]{:S(2)}) collective-permute-start(bf16[256,256]{1,0:T(8,128)(2,1)S(1)} %bitcast.54), channel_id=1, source_target_pairs={{0,4},{4,8},{8,12},{12,16},{16,20},{20,24},{24,28},{28,0},{1,5},{5... | collective-permute-start | bytes 393224 | tf_op jit(solution)/shard_map/ppermute | solution.py:36
  117.2 10.1 %collective-permute-start.31 = (bf16[256,256]{1,0:T(8,128)(2,1)S(1)}, bf16[256,256]{1,0:T(8,128)(2,1)S(1)}, u32[]{:S(2)}, u32[]{:S(2)}) collective-permute-start(bf16[256,256]{1,0:T(8,128)(2,1)S(1)} %bitcast.55), channel_id=1, source_target_pairs={{0,24},{4,28},{8,0},{12,4},{16,8},{20,12},{24,16},{28,20},{1,25},{... | collective-permute-start | bytes 393224 | tf_op jit(solution)/shard_map/ppermute | solution.py:36
  121.5 10.1 %collective-permute-start.32 = (bf16[256,256]{1,0:T(8,128)(2,1)S(1)}, bf16[256,256]{1,0:T(8,128)(2,1)S(1)}, u32[]{:S(2)}, u32[]{:S(2)}) collective-permute-start(bf16[256,256]{1,0:T(8,128)(2,1)S(1)} %bitcast.56), channel_id=1, source_target_pairs={{0,8},{4,12},{8,16},{12,20},{16,24},{20,28},{24,0},{28,4},{1,9},{5... | collective-permute-start | bytes 393224 | tf_op jit(solution)/shard_map/ppermute | solution.py:36
  131.6 6.0 %collective-permute-start.35 = (bf16[128,256]{1,0:T(8,128)(2,1)S(1)}, bf16[128,256]{1,0:T(8,128)(2,1)S(1)}, u32[]{:S(2)}, u32[]{:S(2)}) collective-permute-start(bf16[128,256]{1,0:T(8,128)(2,1)S(1)} %slice.34), channel_id=1, source_target_pairs={{0,24},{4,28},{8,0},{12,4},{16,8},{20,12},{24,16},{28,20},{1,25},{... | collective-permute-start | bytes 196616 | tf_op jit(solution)/shard_map/ppermute | solution.py:36
  133.9 6.6 %collective-permute-start.36 = (bf16[128,256]{1,0:T(8,128)(2,1)S(1)}, bf16[128,256]{1,0:T(8,128)(2,1)S(1)}, u32[]{:S(2)}, u32[]{:S(2)}) collective-permute-start(bf16[128,256]{1,0:T(8,128)(2,1)S(1)} %slice.35), channel_id=1, source_target_pairs={{0,8},{4,12},{8,16},{12,20},{16,24},{20,28},{24,0},{28,4},{1,9},{5... | collective-permute-start | bytes 196616 | tf_op jit(solution)/shard_map/ppermute | solution.py:36
  134.6 6.0 %collective-permute-start.33 = (bf16[256,256]{1,0:T(8,128)(2,1)S(1)}, bf16[256,256]{1,0:T(8,128)(2,1)S(1)}, u32[]{:S(2)}, u32[]{:S(2)}) collective-permute-start(bf16[256,256]{1,0:T(8,128)(2,1)S(1)} %collective-permute-done.31.refs_2_), channel_id=1, source_target_pairs={{0,28},{4,0},{8,4},{12,8},{16,12},{20,16},{24,20},{28,24},{1,29},{... | collective-permute-start | bytes 393224 | tf_op jit(solution)/shard_map/ppermute | solution.py:36
  137.0 6.2 %collective-permute-start.34 = (bf16[256,256]{1,0:T(8,128)(2,1)S(1)}, bf16[256,256]{1,0:T(8,128)(2,1)S(1)}, u32[]{:S(2)}, u32[]{:S(2)}) collective-permute-start(bf16[256,256]{1,0:T(8,128)(2,1)S(1)} %collective-permute-done.32.refs_4_), channel_id=1, source_target_pairs={{0,4},{4,8},{8,12},{12,16},{16,20},{20,24},{24,28},{28,0},{1,5},{5... | collective-permute-start | bytes 393224 | tf_op jit(solution)/shard_map/ppermute | solution.py:36
  145.6 5.0 %collective-permute-start.39 = (bf16[256,256]{1,0:T(8,128)(2,1)S(1)}, bf16[256,256]{1,0:T(8,128)(2,1)S(1)}, u32[]{:S(2)}, u32[]{:S(2)}) collective-permute-start(bf16[256,256]{1,0:T(8,128)(2,1)S(1)} %get-tuple-element.111), channel_id=1, source_target_pairs={{0,1},{1,2},{2,3},{3,0},{4,5},{5,6},{6,7},{7,4},{8,9},{9,10},{10,1... | collective-permute-start | bytes 393224 | tf_op jit(solution)/shard_map/ppermute | solution.py:36
  146.7 6.5 %collective-permute-start.40 = (bf16[256,256]{1,0:T(8,128)(2,1)S(1)}, bf16[256,256]{1,0:T(8,128)(2,1)S(1)}, u32[]{:S(2)}, u32[]{:S(2)}) collective-permute-start(bf16[256,256]{1,0:T(8,128)(2,1)S(1)} %get-tuple-element.113), channel_id=1, source_target_pairs={{0,2},{1,3},{2,0},{3,1},{4,6},{5,7},{6,4},{7,5},{8,10},{9,11},{10,... | collective-permute-start | bytes 393224 | tf_op jit(solution)/shard_map/ppermute | solution.py:36
  147.9 6.7 %collective-permute-start.41 = (bf16[256,256]{1,0:T(8,128)(2,1)S(1)}, bf16[256,256]{1,0:T(8,128)(2,1)S(1)}, u32[]{:S(2)}, u32[]{:S(2)}) collective-permute-start(bf16[256,256]{1,0:T(8,128)(2,1)S(1)} %get-tuple-element.112), channel_id=1, source_target_pairs={{0,3},{1,0},{2,1},{3,2},{4,7},{5,4},{6,5},{7,6},{8,11},{9,8},{10,9... | collective-permute-start | bytes 393224 | tf_op jit(solution)/shard_map/ppermute | solution.py:36
  (9 other events, 88.7 us)

commit v2 on v1

--- a/solution.py
+++ b/solution.py
@@ -450,6 +450,7 @@
     pieces = [piece[0] for piece in pieces] + [piece[1] for piece in pieces]
 
     gated = filtered(where, pieces, spectrum, skip)
+    gated, rows[2] = together(gated, rows[2])
     gated = over_ctx(gated).reshape(256, 256).T
     rows, _ = together(rows, gated)
     rows = jnp.stack(rows)

time: 156 us -> 155 us (level)
  waiting for transfers between devices: 44.2 us -> 40.8 us
  starting transfers between devices: 74.7 us -> 76.9 us
    ppermute x41, waiting for transfers between devices: 44.2 us -> 40.8 us  [shift(): return lax.ppermute(values, axis, [(i, (i + step) % n) for i in range(n)])]
    ppermute x41, starting transfers between devices: 61.4 us -> 63.6 us  [shift(): return lax.ppermute(values, axis, [(i, (i + step) % n) for i in range(n)])]
  transfers between devices with their start and end apart: 43 -> 43, of which waited for: 20 -> 22; matrix products, arithmetic and copies ran while one was open for 4% -> 4% of each run, Pallas kernels for 10% -> 10%
where the time goes in v2:
time: 155 us; the launch traced here: 154 us
  starting transfers between devices  76.9 us (50%)
  waiting for transfers between devices  40.8 us (26%)
  Pallas kernels  17.9 us (12%)
  blocking collectives  10.1 us (7%)
  local copies, waits for them, and re-layouts  3.94 us (3%)
  other arithmetic  2.48 us (2%)
  matrix products  1.77 us (1%)
    ppermute x41, starting transfers between devices, shift(): return lax.ppermute(values, axis, [(i, (i + step) % n) for i in range(n)])  63.6 us
    ppermute x41, waiting for transfers between devices, shift(): return lax.ppermute(values, axis, [(i, (i + step) % n) for i in range(n)])  40.8 us
    all_to_all x1, starting transfers between devices, over_ctx(): return lax.all_to_all(values, CTX, split_axis=0, concat_axis=0, tiled=True)  11.8 us
    all_to_all x1, blocking collectives, over_ctx(): return lax.all_to_all(values, CTX, split_axis=0, concat_axis=0, tiled=True)  10.1 us
    pallas_call x2, Pallas kernels, slot(): pl.pallas_call(functools.partial(slot_kernel, blocks, len(names)), out_sh...  6.24 us
    pallas_call x1, Pallas kernels, filtered(): pl.pallas_call(filter_kernel, out_shape=jax.ShapeDtypeStruct((8, 32, 256)...  3.73 us
    pallas_call x1, Pallas kernels, turned_weight(): pl.pallas_call(turn_kernel, out_shape=jax.ShapeDtypeStruct((2, 768, 1024)...  3.53 us
  transfers between devices with their start and end apart: 43, of which 22 were waited for; matrix products, arithmetic and copies ran while one was open for 4% of the time, Pallas kernels for 10%

profile of v2, /device:TPU:24, one launch (start us, length us, event | category | flops | bytes accessed | tf_op | source)
XLA Modules:
  0.0 154.2 jit_solution(4182665105028432643)
XLA Ops:
  0.0 1.6 %collective-permute-start = (bf16[256,256]{1,0:T(8,128)(2,1)}, bf16[256,256]{1,0:T(8,128)(2,1)S(1)}, u32[]{:S(2)}, u32[]{:S(2)}) collective-permute-start(bf16[256,256]{1,0:T(8,128)(2,1)} %param.10), channel_id=1, source_target_pairs={{0,0},{1,1},{2,2},{3,3},{4,4},{5,5},{6,6},{7,7},{8,64},{9,65},{10,... | collective-permute-start | bytes 393224 | tf_op jit(solution)/shard_map/ppermute | solution.py:395
  1.6 1.8 %convolution_convert_fusion = bf16[2,256,2,256]{1,3,2,0:T(8,128)(2,1)S(1)} fusion(bf16[256,256]{1,0:T(8,128)(2,1)} %constant.203, bf16[256,256]{1,0:T(8,128)(2,1)} %constant.204, pred[2]{0:T(512)(128)(4,1)S(1)} %add_compare_fusion, f32[2,2,256,256]{3,2,1,0:T(8,128)} %param.12), kind=kOutput, calls=%fused_computation.1 | convolution fusion | flops 134873088 | bytes 1835010 | tf_op jit(solution)/shard_map/plgc,lgh->plch/dot_general | solution.py:187
  4.2 11.8 %all-to-all-start = ((bf16[8,2,2,32,256]{4,3,2,1,0:T(8,128)(2,1)}), bf16[8,2,2,32,256]{4,3,2,1,0:T(8,128)(2,1)S(1)}, u32[]{:S(2)}, u32[]{:S(2)}) async-start(bf16[8,2,2,32,256]{4,3,2,1,0:T(8,128)(2,1)} %bitcast.52), calls=%async_computation | async-start | bytes 1048576 | tf_op jit(solution)/shard_map/all_to_all | solution.py:387
  17.8 2.2 %collective-permute-start.3 = (bf16[256,256]{1,0:T(8,128)(2,1)S(1)}, bf16[256,256]{1,0:T(8,128)(2,1)}, u32[]{:S(2)}, u32[]{:S(2)}) collective-permute-start(bf16[256,256]{1,0:T(8,128)(2,1)S(1)} %collective-permute-done.refs_0_), channel_id=1, source_target_pairs={{0,1},{1,2},{2,3},{3,0},{4,5},{5,6},{6,7},{7,4},{8,9},{9,10},{10,1... | collective-permute-start | bytes 393224 | tf_op jit(solution)/shard_map/ppermute | solution.py:36
  20.0 2.7 %dynamic-slice_bitcast_fusion = (bf16[4,256,256]{2,1,0:T(8,128)(2,1)}, bf16[4,256,256]{2,1,0:T(8,128)(2,1)S(1)}, bf16[4,256,256]{2,1,0:T(8,128)(2,1)}, bf16[4,256,256]{2,1,0:T(8,128)(2,1)S(1)}) fusion(bf16[2,4,4,256,256]{4,3,2,1,0:T(8,128)(2,1)} %bitcast.61, s32[]{:T(128)S(6)} %select_n.56, s32[]{:T(128)S(6)} %select_n.68, s32[]{:T(128)S(6)} %select_n.65, ...), kind=kLoop, calls=%fused_computation.4 | loop fusion | bytes 4194324 | tf_op jit(solution)/shard_map/jit(dynamic_index_in_dim)/squeeze | solution.py:407
  22.7 3.4 %collective-permute-done.1.refs_1_ = bf16[256,256]{1,0:T(8,128)(2,1)S(1)} collective-permute-done((bf16[256,256]{1,0:T(8,128)(2,1)S(1)}, bf16[256,256]{1,0:T(8,128)(2,1)S(1)}, u32[]{:S(2)}, u32[]{:S(2)}) %collective-permute-start.1) | collective-permute-done | bytes 131104 | tf_op jit(solution)/shard_map/ppermute | solution.py:36
  26.8 1.9 %shard_map.100 = (bf16[128,1024]{1,0:T(8,128)(2,1)}, bf16[128,1024]{1,0:T(8,128)(2,1)}) custom-call(bf16[256,256]{1,0:T(8,128)(2,1)} %copy-done.11, bf16[256,256]{1,0:T(8,128)(2,1)} %copy-done.12, bf16[256,256]{1,0:T(8,128)(2,1)} %copy-done.13, bf16[256,256]{1,0:T(8,128)(2,1)} %collective-permute-done.3.refs_3_), custom_call_target="tpu_custom_call" | custom-call | flops 2000000000 | bytes 6000000 | tf_op jit(solution)/shard_map/pallas_call | solution.py:272
  29.8 2.2 %collective-permute-start.5 = (bf16[128,1024]{1,0:T(8,128)(2,1)}, bf16[128,1024]{1,0:T(8,128)(2,1)S(1)}, u32[]{:S(2)}, u32[]{:S(2)}) collective-permute-start(bf16[128,1024]{1,0:T(8,128)(2,1)} %get-tuple-element.62.refs_5_), channel_id=1, source_target_pairs={{0,28},{4,0},{8,4},{12,8},{16,12},{20,16},{24,20},{28,24},{1,29},{... | collective-permute-start | bytes 786440 | tf_op jit(solution)/shard_map/ppermute | solution.py:36
  32.0 4.9 %collective-permute-start.4 = (bf16[128,1024]{1,0:T(8,128)(2,1)}, bf16[128,1024]{1,0:T(8,128)(2,1)S(1)}, u32[]{:S(2)}, u32[]{:S(2)}) collective-permute-start(bf16[128,1024]{1,0:T(8,128)(2,1)} %get-tuple-element.61.refs_4_), channel_id=1, source_target_pairs={{0,28},{4,0},{8,4},{12,8},{16,12},{20,16},{24,20},{28,24},{1,29},{... | collective-permute-start | bytes 786440 | tf_op jit(solution)/shard_map/ppermute | solution.py:36
  36.9 2.4 %collective-permute-done.10.refs_6_ = bf16[128,1024]{1,0:T(8,128)(2,1)S(1)} collective-permute-done((bf16[128,1024]{1,0:T(8,128)(2,1)}, bf16[128,1024]{1,0:T(8,128)(2,1)S(1)}, u32[]{:S(2)}, u32[]{:S(2)}) %collective-permute-start.10) | collective-permute-done | bytes 262176 | tf_op jit(solution)/shard_map/ppermute | solution.py:36
  40.0 3.5 %shard_map.101.refs_10_ = bf16[2,768,1024]{2,1,0:T(8,128)(2,1)S(1)} custom-call(s32[4]{0:T(128)S(1)} %pad_add_fusion.place_ref, bf16[3,4,256,256]{3,2,1,0:T(8,128)(2,1)S(1)} %bitcast.58, bf16[3,4,256,256]{3,2,1,0:T(8,128)(2,1)} %bitcast.16.sibling_ref), custom_call_target="tpu_custom_call" | custom-call | flops 3000000000 | bytes 9000000 | tf_op jit(solution)/shard_map/pallas_call | solution.py:238
  43.5 1.4 collective-permute-done.8.refs_7_
  45.0 4.9 %collective-permute-start.9 = (bf16[128,1024]{1,0:T(8,128)(2,1)S(1)}, bf16[128,1024]{1,0:T(8,128)(2,1)S(1)}, u32[]{:S(2)}, u32[]{:S(2)}) collective-permute-start(bf16[128,1024]{1,0:T(8,128)(2,1)S(1)} %collective-permute-done.5.refs_1_), channel_id=1, source_target_pairs={{0,28},{4,0},{8,4},{12,8},{16,12},{20,16},{24,20},{28,24},{1,29},{... | collective-permute-start | bytes 786440 | tf_op jit(solution)/shard_map/ppermute | solution.py:36
  49.9 2.0 %collective-permute-start.6 = (bf16[128,1024]{1,0:T(8,128)(2,1)S(1)}, bf16[128,1024]{1,0:T(8,128)(2,1)S(1)}, u32[]{:S(2)}, u32[]{:S(2)}) collective-permute-start(bf16[128,1024]{1,0:T(8,128)(2,1)S(1)} %collective-permute-done.4.refs_0_), channel_id=1, source_target_pairs={{0,28},{4,0},{8,4},{12,8},{16,12},{20,16},{24,20},{28,24},{1,29},{... | collective-permute-start | bytes 786440 | tf_op jit(solution)/shard_map/ppermute | solution.py:36
  52.4 4.5 %collective-permute-done.12.refs_9_.refs_7_ = bf16[128,1024]{1,0:T(8,128)(2,1)S(1)} collective-permute-done((bf16[128,1024]{1,0:T(8,128)(2,1)S(1)}, bf16[128,1024]{1,0:T(8,128)(2,1)S(1)}, u32[]{:S(2)}, u32[]{:S(2)}) %collective-permute-start.12) | collective-permute-done | bytes 262176 | tf_op jit(solution)/shard_map/ppermute | solution.py:36
  57.0 2.2 %collective-permute-start.14 = (bf16[4,256,256]{2,1,0:T(8,128)(2,1)S(1)}, bf16[4,256,256]{2,1,0:T(8,128)(2,1)S(1)}, u32[]{:S(2)}, u32[]{:S(2)}) collective-permute-start(bf16[4,256,256]{2,1,0:T(8,128)(2,1)S(1)} %copy-done.10), channel_id=1, source_target_pairs={{0,1},{1,2},{2,3},{3,0},{4,5},{5,6},{6,7},{7,4},{8,9},{9,10},{10,1... | collective-permute-start | bytes 1572872 | tf_op jit(solution)/shard_map/ppermute | solution.py:36
  59.1 4.6 %collective-permute-start.17 = (bf16[128,1024]{1,0:T(8,128)(2,1)S(1)}, bf16[128,1024]{1,0:T(8,128)(2,1)S(1)}, u32[]{:S(2)}, u32[]{:S(2)}) collective-permute-start(bf16[128,1024]{1,0:T(8,128)(2,1)S(1)} %collective-permute-done.6.refs_2_), channel_id=1, source_target_pairs={{0,28},{4,0},{8,4},{12,8},{16,12},{20,16},{24,20},{28,24},{1,29},{... | collective-permute-start | bytes 786440 | tf_op jit(solution)/shard_map/ppermute | solution.py:36
  63.7 3.2 %collective-permute-start.15 = (bf16[128,1024]{1,0:T(8,128)(2,1)S(1)}, bf16[128,1024]{1,0:T(8,128)(2,1)S(1)}, u32[]{:S(2)}, u32[]{:S(2)}) collective-permute-start(bf16[128,1024]{1,0:T(8,128)(2,1)S(1)} %collective-permute-done.9.refs_3_), channel_id=1, source_target_pairs={{0,28},{4,0},{8,4},{12,8},{16,12},{20,16},{24,20},{28,24},{1,29},{... | collective-permute-start | bytes 786440 | tf_op jit(solution)/shard_map/ppermute | solution.py:36
  67.0 3.1 %shard_map.102 = (f32[192,512]{1,0:T(8,128)S(1)}, bf16[192,512]{1,0:T(8,128)(2,1)S(1)}, bf16[192,512]{1,0:T(8,128)(2,1)S(1)}, bf16[192,512]{1,0:T(8,128)(2,1)S(1)}) custom-call(s32[4]{0:T(128)S(1)} %pad_add_fusion.place_ref, bf16[128,1024]{1,0:T(8,128)(2,1)S(1)} %collective-permute-done.4.refs_0_, bf16[128,1024]{1,0:T(8,128)(2,1)S(1)} %collective-permute-done.5.refs_1_, ...), custom_call_target="tpu_custom_call" | custom-call | flops 3000000000 | bytes 9000000 | tf_op jit(solution)/shard_map/pallas_call | solution.py:323
  70.1 2.2 %collective-permute-done.15.refs_5_ = bf16[128,1024]{1,0:T(8,128)(2,1)S(1)} collective-permute-done((bf16[128,1024]{1,0:T(8,128)(2,1)S(1)}, bf16[128,1024]{1,0:T(8,128)(2,1)S(1)}, u32[]{:S(2)}, u32[]{:S(2)}) %collective-permute-start.15) | collective-permute-done | bytes 262176 | tf_op jit(solution)/shard_map/ppermute | solution.py:36
  72.3 3.7 %collective-permute-start.20 = (bf16[128,1024]{1,0:T(8,128)(2,1)S(1)}, bf16[128,1024]{1,0:T(8,128)(2,1)S(1)}, u32[]{:S(2)}, u32[]{:S(2)}) collective-permute-start(bf16[128,1024]{1,0:T(8,128)(2,1)S(1)} %collective-permute-done.15.refs_5_), channel_id=1, source_target_pairs={{0,28},{4,0},{8,4},{12,8},{16,12},{20,16},{24,20},{28,24},{1,29},{... | collective-permute-start | bytes 786440 | tf_op jit(solution)/shard_map/ppermute | solution.py:36
  76.0 2.0 %collective-permute-start.22 = (bf16[192,512]{1,0:T(8,128)(2,1)S(1)}, bf16[192,512]{1,0:T(8,128)(2,1)S(1)}, u32[]{:S(2)}, u32[]{:S(2)}) collective-permute-start(bf16[192,512]{1,0:T(8,128)(2,1)S(1)} %get-tuple-element.86), channel_id=1, source_target_pairs={{0,128},{64,192},{128,0},{192,64},{1,129},{65,193},{129,1},{193,65... | collective-permute-start | bytes 589832 | tf_op jit(solution)/shard_map/ppermute | solution.py:36
  78.0 2.5 %collective-permute-start.23 = (bf16[192,512]{1,0:T(8,128)(2,1)S(1)}, bf16[192,512]{1,0:T(8,128)(2,1)S(1)}, u32[]{:S(2)}, u32[]{:S(2)}) collective-permute-start(bf16[192,512]{1,0:T(8,128)(2,1)S(1)} %get-tuple-element.87), channel_id=1, source_target_pairs={{0,192},{64,0},{128,64},{192,128},{1,193},{65,1},{129,65},{193,129... | collective-permute-start | bytes 589832 | tf_op jit(solution)/shard_map/ppermute | solution.py:36
  80.5 3.1 %shard_map.103 = (f32[192,512]{1,0:T(8,128)S(1)}, bf16[192,512]{1,0:T(8,128)(2,1)S(1)}, bf16[192,512]{1,0:T(8,128)(2,1)S(1)}, bf16[192,512]{1,0:T(8,128)(2,1)S(1)}) custom-call(s32[4]{0:T(128)S(1)} %pad_add_fusion.place_ref, bf16[128,1024]{1,0:T(8,128)(2,1)S(1)} %collective-permute-done.19.refs_0_, bf16[128,1024]{1,0:T(8,128)(2,1)S(1)} %collective-permute-done.20.refs_1_, ...), custom_call_target="tpu_custom_call" | custom-call | flops 3000000000 | bytes 9000000 | tf_op jit(solution)/shard_map/pallas_call | solution.py:323
  83.6 1.4 collective-permute-start.29
  85.7 1.1 collective-permute-done.23
  86.8 2.8 %collective-permute-start.24 = (bf16[192,512]{1,0:T(8,128)(2,1)S(1)}, bf16[192,512]{1,0:T(8,128)(2,1)S(1)}, u32[]{:S(2)}, u32[]{:S(2)}) collective-permute-start(bf16[192,512]{1,0:T(8,128)(2,1)S(1)} %get-tuple-element.92), channel_id=1, source_target_pairs={{0,64},{64,128},{128,192},{192,0},{1,65},{65,129},{129,193},{193,1... | collective-permute-start | bytes 589832 | tf_op jit(solution)/shard_map/ppermute | solution.py:36
  89.6 1.4 collective-permute-start.25
  91.0 1.4 collective-permute-start.26
  93.7 3.1 %collective-permute-done.25 = bf16[192,512]{1,0:T(8,128)(2,1)S(1)} collective-permute-done((bf16[192,512]{1,0:T(8,128)(2,1)S(1)}, bf16[192,512]{1,0:T(8,128)(2,1)S(1)}, u32[]{:S(2)}, u32[]{:S(2)}) %collective-permute-start.25) | collective-permute-done | bytes 196640 | tf_op jit(solution)/shard_map/ppermute | solution.py:36
  97.5 1.2 collective-permute-done.28.refs_4_
  98.7 3.7 %shard_map.104 = bf16[8,32,256]{2,1,0:T(8,128)(2,1)S(1)} custom-call(s32[4]{0:T(128)S(1)} %pad_add_fusion.place_ref, f32[32,1]{1,0:T(8,128)S(1)} %copy.25.refs_0_, f32[96,512]{1,0:T(8,128)S(1)} %get-tuple-element.121.refs_1_, f32[96,512]{1,0:T(8,128)S(1)} %get-tuple-element.119.refs_2_, f32[96,512]{1,0:T(8,128)S(1)} %collective-permute-done.27.refs_3_, ...), custom_call_target="tpu_custom_call" | custom-call | flops 3000000000 | bytes 9000000 | tf_op jit(solution)/shard_map/pallas_call | solution.py:158
  102.5 10.1 %all_to_all.10 = bf16[8,32,256]{2,1,0:T(8,128)(2,1)S(1)} all-to-all(bf16[8,32,256]{2,1,0:T(8,128)(2,1)S(1)} %shard_map.104), channel_id=1, replica_groups=mesh['x'=4,'core'=2,'z'=8,'y'=4] {'x','core'}, dimensions={0} | all-to-all | bytes 262144 | tf_op jit(solution)/shard_map/all_to_all | solution.py:387
  112.6 1.5 pad_maximum_fusion.refs_8_
  114.7 1.6 %collective-permute-start.31 = (bf16[256,256]{1,0:T(8,128)(2,1)S(1)}, bf16[256,256]{1,0:T(8,128)(2,1)S(1)}, u32[]{:S(2)}, u32[]{:S(2)}) collective-permute-start(bf16[256,256]{1,0:T(8,128)(2,1)S(1)} %bitcast.54), channel_id=1, source_target_pairs={{0,4},{4,8},{8,12},{12,16},{16,20},{20,24},{24,28},{28,0},{1,5},{5... | collective-permute-start | bytes 393224 | tf_op jit(solution)/shard_map/ppermute | solution.py:36
  117.0 2.2 %collective-permute-start.33 = (bf16[256,256]{1,0:T(8,128)(2,1)S(1)}, bf16[256,256]{1,0:T(8,128)(2,1)S(1)}, u32[]{:S(2)}, u32[]{:S(2)}) collective-permute-start(bf16[256,256]{1,0:T(8,128)(2,1)S(1)} %bitcast.56), channel_id=1, source_target_pairs={{0,8},{4,12},{8,16},{12,20},{16,24},{20,28},{24,0},{28,4},{1,9},{5... | collective-permute-start | bytes 393224 | tf_op jit(solution)/shard_map/ppermute | solution.py:36
  119.2 3.7 %collective-permute-done.30.refs_1_ = bf16[256,256]{1,0:T(8,128)(2,1)S(1)} collective-permute-done((bf16[256,256]{1,0:T(8,128)(2,1)S(1)}, bf16[256,256]{1,0:T(8,128)(2,1)S(1)}, u32[]{:S(2)}, u32[]{:S(2)}) %collective-permute-start.30) | collective-permute-done | bytes 131104 | tf_op jit(solution)/shard_map/ppermute | solution.py:36
  123.0 1.8 %collective-permute-done.32.refs_2_ = bf16[256,256]{1,0:T(8,128)(2,1)S(1)} collective-permute-done((bf16[256,256]{1,0:T(8,128)(2,1)S(1)}, bf16[256,256]{1,0:T(8,128)(2,1)S(1)}, u32[]{:S(2)}, u32[]{:S(2)}) %collective-permute-start.32) | collective-permute-done | bytes 131104 | tf_op jit(solution)/shard_map/ppermute | solution.py:36
  125.3 2.8 %collective-permute-start.36 = (bf16[128,256]{1,0:T(8,128)(2,1)S(1)}, bf16[128,256]{1,0:T(8,128)(2,1)S(1)}, u32[]{:S(2)}, u32[]{:S(2)}) collective-permute-start(bf16[128,256]{1,0:T(8,128)(2,1)S(1)} %slice.34), channel_id=1, source_target_pairs={{0,24},{4,28},{8,0},{12,4},{16,8},{20,12},{24,16},{28,20},{1,25},{... | collective-permute-start | bytes 196616 | tf_op jit(solution)/shard_map/ppermute | solution.py:36
  128.1 2.9 %collective-permute-start.37 = (bf16[128,256]{1,0:T(8,128)(2,1)S(1)}, bf16[128,256]{1,0:T(8,128)(2,1)S(1)}, u32[]{:S(2)}, u32[]{:S(2)}) collective-permute-start(bf16[128,256]{1,0:T(8,128)(2,1)S(1)} %slice.35), channel_id=1, source_target_pairs={{0,8},{4,12},{8,16},{12,20},{16,24},{20,28},{24,0},{28,4},{1,9},{5... | collective-permute-start | bytes 196616 | tf_op jit(solution)/shard_map/ppermute | solution.py:36
  131.0 3.7 %collective-permute-start.34 = (bf16[256,256]{1,0:T(8,128)(2,1)S(1)}, bf16[256,256]{1,0:T(8,128)(2,1)S(1)}, u32[]{:S(2)}, u32[]{:S(2)}) collective-permute-start(bf16[256,256]{1,0:T(8,128)(2,1)S(1)} %collective-permute-done.32.refs_2_), channel_id=1, source_target_pairs={{0,28},{4,0},{8,4},{12,8},{16,12},{20,16},{24,20},{28,24},{1,29},{... | collective-permute-start | bytes 393224 | tf_op jit(solution)/shard_map/ppermute | solution.py:36
  135.5 1.8 %collective-permute-done.34.refs_5_ = bf16[256,256]{1,0:T(8,128)(2,1)S(1)} collective-permute-done((bf16[256,256]{1,0:T(8,128)(2,1)S(1)}, bf16[256,256]{1,0:T(8,128)(2,1)S(1)}, u32[]{:S(2)}, u32[]{:S(2)}) %collective-permute-start.34) | collective-permute-done | bytes 131104 | tf_op jit(solution)/shard_map/ppermute | solution.py:36
  137.3 3.6 %collective-permute-done.35.refs_6_ = bf16[256,256]{1,0:T(8,128)(2,1)S(1)} collective-permute-done((bf16[256,256]{1,0:T(8,128)(2,1)S(1)}, bf16[256,256]{1,0:T(8,128)(2,1)S(1)}, u32[]{:S(2)}, u32[]{:S(2)}) %collective-permute-start.35) | collective-permute-done | bytes 131104 | tf_op jit(solution)/shard_map/ppermute | solution.py:36
  140.9 2.4 %shard_map.105 = bf16[4,256,256]{2,1,0:T(8,128)(2,1)S(1)} custom-call(s32[4]{0:T(128)S(1)} %pad_add_fusion.place_ref, bf16[256,256]{1,0:T(8,128)(2,1)S(1)} %bitcast.57, bf16[256,256]{1,0:T(8,128)(2,1)S(1)} %collective-permute-done.30.refs_1_, bf16[256,256]{1,0:T(8,128)(2,1)S(1)} %collective-permute-done.32.refs_2_, ...), custom_call_target="tpu_custom_call" | custom-call | flops 2000000000 | bytes 6000000 | tf_op jit(solution)/shard_map/pallas_call | solution.py:375
  143.4 2.5 %collective-permute-start.39 = (bf16[256,256]{1,0:T(8,128)(2,1)S(1)}, bf16[256,256]{1,0:T(8,128)(2,1)S(1)}, u32[]{:S(2)}, u32[]{:S(2)}) collective-permute-start(bf16[256,256]{1,0:T(8,128)(2,1)S(1)} %get-tuple-element.115), channel_id=1, source_target_pairs={{0,1},{1,2},{2,3},{3,0},{4,5},{5,6},{6,7},{7,4},{8,9},{9,10},{10,1... | collective-permute-start | bytes 393224 | tf_op jit(solution)/shard_map/ppermute | solution.py:36
  145.8 1.3 collective-permute-start.41
  147.2 2.6 %collective-permute-done.39 = bf16[256,256]{1,0:T(8,128)(2,1)S(1)} collective-permute-done((bf16[256,256]{1,0:T(8,128)(2,1)S(1)}, bf16[256,256]{1,0:T(8,128)(2,1)S(1)}, u32[]{:S(2)}, u32[]{:S(2)}) %collective-permute-start.39) | collective-permute-done | bytes 131104 | tf_op jit(solution)/shard_map/ppermute | solution.py:36
  149.7 2.7 %collective-permute-done.40 = bf16[256,256]{1,0:T(8,128)(2,1)S(1)} collective-permute-done((bf16[256,256]{1,0:T(8,128)(2,1)S(1)}, bf16[256,256]{1,0:T(8,128)(2,1)S(1)}, u32[]{:S(2)}, u32[]{:S(2)}) %collective-permute-start.40) | collective-permute-done | bytes 131104 | tf_op jit(solution)/shard_map/ppermute | solution.py:36
  (91 shorter events, 12.7 us)
Async XLA Ops:
  0.0 97.3 %copy-start = (f32[256]{0:T(256)S(1)}, f32[256]{0:T(256)}, u32[]{:S(2)}) copy-start(f32[256]{0:T(256)} %param.13) | copy-start | bytes 3076
  0.0 39.9 %collective-permute-start.7 = (bf16[3,1024,256]{2,1,0:T(8,128)(2,1)}, bf16[3,1024,256]{2,1,0:T(8,128)(2,1)}, u32[]{:S(2)}, u32[]{:S(2)}) collective-permute-start(bf16[3,1024,256]{2,1,0:T(8,128)(2,1)} %param.11), channel_id=1, source_target_pairs={{0,32},{32,0},{1,33},{33,1},{2,34},{34,2},{3,35},{35,3},{4,36},{36... | collective-permute-start | bytes 4718600 | tf_op jit(solution)/shard_map/ppermute | solution.py:36
  0.0 16.0 %collective-permute-start = (bf16[256,256]{1,0:T(8,128)(2,1)}, bf16[256,256]{1,0:T(8,128)(2,1)S(1)}, u32[]{:S(2)}, u32[]{:S(2)}) collective-permute-start(bf16[256,256]{1,0:T(8,128)(2,1)} %param.10), channel_id=1, source_target_pairs={{0,0},{1,1},{2,2},{3,3},{4,4},{5,5},{6,6},{7,7},{8,64},{9,65},{10,... | collective-permute-start | bytes 393224 | tf_op jit(solution)/shard_map/ppermute | solution.py:395
  4.2 24.5 %all-to-all-start = ((bf16[8,2,2,32,256]{4,3,2,1,0:T(8,128)(2,1)}), bf16[8,2,2,32,256]{4,3,2,1,0:T(8,128)(2,1)S(1)}, u32[]{:S(2)}, u32[]{:S(2)}) async-start(bf16[8,2,2,32,256]{4,3,2,1,0:T(8,128)(2,1)} %bitcast.52), calls=%async_computation | async-start | bytes 1048576 | tf_op jit(solution)/shard_map/all_to_all | solution.py:387
  16.0 10.0 %collective-permute-start.1 = (bf16[256,256]{1,0:T(8,128)(2,1)S(1)}, bf16[256,256]{1,0:T(8,128)(2,1)S(1)}, u32[]{:S(2)}, u32[]{:S(2)}) collective-permute-start(bf16[256,256]{1,0:T(8,128)(2,1)S(1)} %collective-permute-done.refs_0_), channel_id=1, source_target_pairs={{0,3},{1,0},{2,1},{3,2},{4,7},{5,4},{6,5},{7,6},{8,11},{9,8},{10,9... | collective-permute-start | bytes 393224 | tf_op jit(solution)/shard_map/ppermute | solution.py:36
  16.9 9.2 %collective-permute-start.2 = (bf16[256,256]{1,0:T(8,128)(2,1)S(1)}, bf16[256,256]{1,0:T(8,128)(2,1)S(1)}, u32[]{:S(2)}, u32[]{:S(2)}) collective-permute-start(bf16[256,256]{1,0:T(8,128)(2,1)S(1)} %collective-permute-done.refs_0_), channel_id=1, source_target_pairs={{0,2},{1,3},{2,0},{3,1},{4,6},{5,7},{6,4},{7,5},{8,10},{9,11},{10,... | collective-permute-start | bytes 393224 | tf_op jit(solution)/shard_map/ppermute | solution.py:36
  17.8 9.0 %collective-permute-start.3 = (bf16[256,256]{1,0:T(8,128)(2,1)S(1)}, bf16[256,256]{1,0:T(8,128)(2,1)}, u32[]{:S(2)}, u32[]{:S(2)}) collective-permute-start(bf16[256,256]{1,0:T(8,128)(2,1)S(1)} %collective-permute-done.refs_0_), channel_id=1, source_target_pairs={{0,1},{1,2},{2,3},{3,0},{4,5},{5,6},{6,7},{7,4},{8,9},{9,10},{10,1... | collective-permute-start | bytes 393224 | tf_op jit(solution)/shard_map/ppermute | solution.py:36
  22.7 17.3 %copy-start.1 = (bf16[3,1024,256]{2,1,0:T(8,128)(2,1)S(1)}, bf16[3,1024,256]{2,1,0:T(8,128)(2,1)}, u32[]{:S(2)}) copy-start(bf16[3,1024,256]{2,1,0:T(8,128)(2,1)} %param.11) | copy-start | bytes 4718596
  28.7 10.6 %collective-permute-start.10 = (bf16[128,1024]{1,0:T(8,128)(2,1)}, bf16[128,1024]{1,0:T(8,128)(2,1)S(1)}, u32[]{:S(2)}, u32[]{:S(2)}) collective-permute-start(bf16[128,1024]{1,0:T(8,128)(2,1)} %get-tuple-element.61.refs_4_), channel_id=1, source_target_pairs={{0,4},{4,8},{8,12},{12,16},{16,20},{20,24},{24,28},{28,0},{1,5},{5... | collective-permute-start | bytes 786440 | tf_op jit(solution)/shard_map/ppermute | solution.py:36
  29.8 13.7 %collective-permute-start.5 = (bf16[128,1024]{1,0:T(8,128)(2,1)}, bf16[128,1024]{1,0:T(8,128)(2,1)S(1)}, u32[]{:S(2)}, u32[]{:S(2)}) collective-permute-start(bf16[128,1024]{1,0:T(8,128)(2,1)} %get-tuple-element.62.refs_5_), channel_id=1, source_target_pairs={{0,28},{4,0},{8,4},{12,8},{16,12},{20,16},{24,20},{28,24},{1,29},{... | collective-permute-start | bytes 786440 | tf_op jit(solution)/shard_map/ppermute | solution.py:36
  32.0 12.9 %collective-permute-start.8 = (bf16[128,1024]{1,0:T(8,128)(2,1)}, bf16[128,1024]{1,0:T(8,128)(2,1)S(1)}, u32[]{:S(2)}, u32[]{:S(2)}) collective-permute-start(bf16[128,1024]{1,0:T(8,128)(2,1)} %get-tuple-element.62.refs_5_), channel_id=1, source_target_pairs={{0,4},{4,8},{8,12},{12,16},{16,20},{20,24},{24,28},{28,0},{1,5},{5... | collective-permute-start | bytes 786440 | tf_op jit(solution)/shard_map/ppermute | solution.py:36
  32.0 17.8 %collective-permute-start.4 = (bf16[128,1024]{1,0:T(8,128)(2,1)}, bf16[128,1024]{1,0:T(8,128)(2,1)S(1)}, u32[]{:S(2)}, u32[]{:S(2)}) collective-permute-start(bf16[128,1024]{1,0:T(8,128)(2,1)} %get-tuple-element.61.refs_4_), channel_id=1, source_target_pairs={{0,28},{4,0},{8,4},{12,8},{16,12},{20,16},{24,20},{28,24},{1,29},{... | collective-permute-start | bytes 786440 | tf_op jit(solution)/shard_map/ppermute | solution.py:36
  39.3 13.1 %collective-permute-start.13 = (bf16[4,256,256]{2,1,0:T(8,128)(2,1)}, bf16[4,256,256]{2,1,0:T(8,128)(2,1)S(1)}, u32[]{:S(2)}, u32[]{:S(2)}) collective-permute-start(bf16[4,256,256]{2,1,0:T(8,128)(2,1)} %get-tuple-element.70), channel_id=1, source_target_pairs={{0,3},{1,0},{2,1},{3,2},{4,7},{5,4},{6,5},{7,6},{8,11},{9,8},{10,9... | collective-permute-start | bytes 1572872 | tf_op jit(solution)/shard_map/ppermute | solution.py:36
  39.9 12.0 %collective-permute-start.11 = (bf16[128,1024]{1,0:T(8,128)(2,1)S(1)}, bf16[128,1024]{1,0:T(8,128)(2,1)S(1)}, u32[]{:S(2)}, u32[]{:S(2)}) collective-permute-start(bf16[128,1024]{1,0:T(8,128)(2,1)S(1)} %collective-permute-done.10.refs_6_), channel_id=1, source_target_pairs={{0,4},{4,8},{8,12},{12,16},{16,20},{20,24},{24,28},{28,0},{1,5},{5... | collective-permute-start | bytes 786440 | tf_op jit(solution)/shard_map/ppermute | solution.py:36
  39.9 27.0 %copy-start.2 = (bf16[128,1024]{1,0:T(8,128)(2,1)S(1)}, bf16[128,1024]{1,0:T(8,128)(2,1)}, u32[]{:S(2)}) copy-start(bf16[128,1024]{1,0:T(8,128)(2,1)} %get-tuple-element.61.refs_4_) | copy-start | bytes 786436
  39.9 27.0 %copy-start.3 = (bf16[128,1024]{1,0:T(8,128)(2,1)S(1)}, bf16[128,1024]{1,0:T(8,128)(2,1)}, u32[]{:S(2)}) copy-start(bf16[128,1024]{1,0:T(8,128)(2,1)} %get-tuple-element.62.refs_5_) | copy-start | bytes 786436
  45.0 12.0 %collective-permute-start.12 = (bf16[128,1024]{1,0:T(8,128)(2,1)S(1)}, bf16[128,1024]{1,0:T(8,128)(2,1)S(1)}, u32[]{:S(2)}, u32[]{:S(2)}) collective-permute-start(bf16[128,1024]{1,0:T(8,128)(2,1)S(1)} %collective-permute-done.8.refs_7_), channel_id=1, source_target_pairs={{0,4},{4,8},{8,12},{12,16},{16,20},{20,24},{24,28},{28,0},{1,5},{5... | collective-permute-start | bytes 786440 | tf_op jit(solution)/shard_map/ppermute | solution.py:36
  45.0 12.0 %collective-permute-start.9 = (bf16[128,1024]{1,0:T(8,128)(2,1)S(1)}, bf16[128,1024]{1,0:T(8,128)(2,1)S(1)}, u32[]{:S(2)}, u32[]{:S(2)}) collective-permute-start(bf16[128,1024]{1,0:T(8,128)(2,1)S(1)} %collective-permute-done.5.refs_1_), channel_id=1, source_target_pairs={{0,28},{4,0},{8,4},{12,8},{16,12},{20,16},{24,20},{28,24},{1,29},{... | collective-permute-start | bytes 786440 | tf_op jit(solution)/shard_map/ppermute | solution.py:36
  49.9 9.3 %collective-permute-start.6 = (bf16[128,1024]{1,0:T(8,128)(2,1)S(1)}, bf16[128,1024]{1,0:T(8,128)(2,1)S(1)}, u32[]{:S(2)}, u32[]{:S(2)}) collective-permute-start(bf16[128,1024]{1,0:T(8,128)(2,1)S(1)} %collective-permute-done.4.refs_0_), channel_id=1, source_target_pairs={{0,28},{4,0},{8,4},{12,8},{16,12},{20,16},{24,20},{28,24},{1,29},{... | collective-permute-start | bytes 786440 | tf_op jit(solution)/shard_map/ppermute | solution.py:36
  51.9 11.8 %collective-permute-start.18 = (bf16[128,1024]{1,0:T(8,128)(2,1)S(1)}, bf16[128,1024]{1,0:T(8,128)(2,1)S(1)}, u32[]{:S(2)}, u32[]{:S(2)}) collective-permute-start(bf16[128,1024]{1,0:T(8,128)(2,1)S(1)} %collective-permute-done.11.refs_8_.refs_6_), channel_id=1, source_target_pairs={{0,4},{4,8},{8,12},{12,16},{16,20},{20,24},{24,28},{28,0},{1,5},{5... | collective-permute-start | bytes 786440 | tf_op jit(solution)/shard_map/ppermute | solution.py:36
  52.4 17.7 %copy-start.7 = (bf16[4,256,256]{2,1,0:T(8,128)(2,1)}, bf16[4,256,256]{2,1,0:T(8,128)(2,1)S(1)}, u32[]{:S(2)}) copy-start(bf16[4,256,256]{2,1,0:T(8,128)(2,1)S(1)} %collective-permute-done.13) | copy-start | bytes 1572868
  57.0 15.4 %collective-permute-start.14 = (bf16[4,256,256]{2,1,0:T(8,128)(2,1)S(1)}, bf16[4,256,256]{2,1,0:T(8,128)(2,1)S(1)}, u32[]{:S(2)}, u32[]{:S(2)}) collective-permute-start(bf16[4,256,256]{2,1,0:T(8,128)(2,1)S(1)} %copy-done.10), channel_id=1, source_target_pairs={{0,1},{1,2},{2,3},{3,0},{4,5},{5,6},{6,7},{7,4},{8,9},{9,10},{10,1... | collective-permute-start | bytes 1572872 | tf_op jit(solution)/shard_map/ppermute | solution.py:36
  59.1 16.9 %collective-permute-start.17 = (bf16[128,1024]{1,0:T(8,128)(2,1)S(1)}, bf16[128,1024]{1,0:T(8,128)(2,1)S(1)}, u32[]{:S(2)}, u32[]{:S(2)}) collective-permute-start(bf16[128,1024]{1,0:T(8,128)(2,1)S(1)} %collective-permute-done.6.refs_2_), channel_id=1, source_target_pairs={{0,28},{4,0},{8,4},{12,8},{16,12},{20,16},{24,20},{28,24},{1,29},{... | collective-permute-start | bytes 786440 | tf_op jit(solution)/shard_map/ppermute | solution.py:36
  63.7 16.8 %collective-permute-start.19 = (bf16[128,1024]{1,0:T(8,128)(2,1)S(1)}, bf16[128,1024]{1,0:T(8,128)(2,1)S(1)}, u32[]{:S(2)}, u32[]{:S(2)}) collective-permute-start(bf16[128,1024]{1,0:T(8,128)(2,1)S(1)} %collective-permute-done.18.refs_8_), channel_id=1, source_target_pairs={{0,4},{4,8},{8,12},{12,16},{16,20},{20,24},{24,28},{28,0},{1,5},{5... | collective-permute-start | bytes 786440 | tf_op jit(solution)/shard_map/ppermute | solution.py:36
  63.7 8.6 %collective-permute-start.15 = (bf16[128,1024]{1,0:T(8,128)(2,1)S(1)}, bf16[128,1024]{1,0:T(8,128)(2,1)S(1)}, u32[]{:S(2)}, u32[]{:S(2)}) collective-permute-start(bf16[128,1024]{1,0:T(8,128)(2,1)S(1)} %collective-permute-done.9.refs_3_), channel_id=1, source_target_pairs={{0,28},{4,0},{8,4},{12,8},{16,12},{20,16},{24,20},{28,24},{1,29},{... | collective-permute-start | bytes 786440 | tf_op jit(solution)/shard_map/ppermute | solution.py:36
  67.0 9.1 %collective-permute-start.16 = (bf16[128,1024]{1,0:T(8,128)(2,1)S(1)}, bf16[128,1024]{1,0:T(8,128)(2,1)S(1)}, u32[]{:S(2)}, u32[]{:S(2)}) collective-permute-start(bf16[128,1024]{1,0:T(8,128)(2,1)S(1)} %collective-permute-done.12.refs_9_.refs_7_), channel_id=1, source_target_pairs={{0,4},{4,8},{8,12},{12,16},{16,20},{20,24},{24,28},{28,0},{1,5},{5... | collective-permute-start | bytes 786440 | tf_op jit(solution)/shard_map/ppermute | solution.py:36
  72.3 8.2 %collective-permute-start.20 = (bf16[128,1024]{1,0:T(8,128)(2,1)S(1)}, bf16[128,1024]{1,0:T(8,128)(2,1)S(1)}, u32[]{:S(2)}, u32[]{:S(2)}) collective-permute-start(bf16[128,1024]{1,0:T(8,128)(2,1)S(1)} %collective-permute-done.15.refs_5_), channel_id=1, source_target_pairs={{0,28},{4,0},{8,4},{12,8},{16,12},{20,16},{24,20},{28,24},{1,29},{... | collective-permute-start | bytes 786440 | tf_op jit(solution)/shard_map/ppermute | solution.py:36
  76.0 9.6 %collective-permute-start.21 = (bf16[192,512]{1,0:T(8,128)(2,1)S(1)}, bf16[192,512]{1,0:T(8,128)(2,1)S(1)}, u32[]{:S(2)}, u32[]{:S(2)}) collective-permute-start(bf16[192,512]{1,0:T(8,128)(2,1)S(1)} %get-tuple-element.85), channel_id=1, source_target_pairs={{0,64},{64,128},{128,192},{192,0},{1,65},{65,129},{129,193},{193,1... | collective-permute-start | bytes 589832 | tf_op jit(solution)/shard_map/ppermute | solution.py:36
  76.0 9.6 %collective-permute-start.22 = (bf16[192,512]{1,0:T(8,128)(2,1)S(1)}, bf16[192,512]{1,0:T(8,128)(2,1)S(1)}, u32[]{:S(2)}, u32[]{:S(2)}) collective-permute-start(bf16[192,512]{1,0:T(8,128)(2,1)S(1)} %get-tuple-element.86), channel_id=1, source_target_pairs={{0,128},{64,192},{128,0},{192,64},{1,129},{65,193},{129,1},{193,65... | collective-permute-start | bytes 589832 | tf_op jit(solution)/shard_map/ppermute | solution.py:36
  78.0 8.8 %collective-permute-start.23 = (bf16[192,512]{1,0:T(8,128)(2,1)S(1)}, bf16[192,512]{1,0:T(8,128)(2,1)S(1)}, u32[]{:S(2)}, u32[]{:S(2)}) collective-permute-start(bf16[192,512]{1,0:T(8,128)(2,1)S(1)} %get-tuple-element.87), channel_id=1, source_target_pairs={{0,192},{64,0},{128,64},{192,128},{1,193},{65,1},{129,65},{193,129... | collective-permute-start | bytes 589832 | tf_op jit(solution)/shard_map/ppermute | solution.py:36
  83.6 18.8 %collective-permute-start.29 = (bf16[4,256,256]{2,1,0:T(8,128)(2,1)S(1)}, bf16[4,256,256]{2,1,0:T(8,128)(2,1)}, u32[]{:S(2)}, u32[]{:S(2)}) collective-permute-start(bf16[4,256,256]{2,1,0:T(8,128)(2,1)S(1)} %get-tuple-element.97), channel_id=1, source_target_pairs={{0,2},{1,3},{2,0},{3,1},{4,6},{5,7},{6,4},{7,5},{8,10},{9,11},{10,... | collective-permute-start | bytes 1572872 | tf_op jit(solution)/shard_map/ppermute | solution.py:36
  86.8 6.9 %collective-permute-start.24 = (bf16[192,512]{1,0:T(8,128)(2,1)S(1)}, bf16[192,512]{1,0:T(8,128)(2,1)S(1)}, u32[]{:S(2)}, u32[]{:S(2)}) collective-permute-start(bf16[192,512]{1,0:T(8,128)(2,1)S(1)} %get-tuple-element.92), channel_id=1, source_target_pairs={{0,64},{64,128},{128,192},{192,0},{1,65},{65,129},{129,193},{193,1... | collective-permute-start | bytes 589832 | tf_op jit(solution)/shard_map/ppermute | solution.py:36
  89.6 7.2 %collective-permute-start.25 = (bf16[192,512]{1,0:T(8,128)(2,1)S(1)}, bf16[192,512]{1,0:T(8,128)(2,1)S(1)}, u32[]{:S(2)}, u32[]{:S(2)}) collective-permute-start(bf16[192,512]{1,0:T(8,128)(2,1)S(1)} %get-tuple-element.93), channel_id=1, source_target_pairs={{0,128},{64,192},{128,0},{192,64},{1,129},{65,193},{129,1},{193,65... | collective-permute-start | bytes 589832 | tf_op jit(solution)/shard_map/ppermute | solution.py:36
  91.0 5.8 %collective-permute-start.26 = (bf16[192,512]{1,0:T(8,128)(2,1)S(1)}, bf16[192,512]{1,0:T(8,128)(2,1)S(1)}, u32[]{:S(2)}, u32[]{:S(2)}) collective-permute-start(bf16[192,512]{1,0:T(8,128)(2,1)S(1)} %get-tuple-element.94), channel_id=1, source_target_pairs={{0,192},{64,0},{128,64},{192,128},{1,193},{65,1},{129,65},{193,129... | collective-permute-start | bytes 589832 | tf_op jit(solution)/shard_map/ppermute | solution.py:36
  92.5 4.9 %collective-permute-start.27 = (f32[96,512]{1,0:T(8,128)S(1)}, f32[96,512]{1,0:T(8,128)S(1)}, u32[]{:S(2)}, u32[]{:S(2)}) collective-permute-start(f32[96,512]{1,0:T(8,128)S(1)} %get-tuple-element.120), channel_id=1, source_target_pairs={{0,32},{32,0},{1,33},{33,1},{2,34},{34,2},{3,35},{35,3},{4,36},{36... | collective-permute-start | bytes 589832 | tf_op jit(solution)/shard_map/ppermute | solution.py:36
  97.0 1.7 %collective-permute-start.28 = (f32[96,512]{1,0:T(8,128)S(1)}, f32[96,512]{1,0:T(8,128)S(1)}, u32[]{:S(2)}, u32[]{:S(2)}) collective-permute-start(f32[96,512]{1,0:T(8,128)S(1)} %get-tuple-element.118), channel_id=1, source_target_pairs={{0,32},{32,0},{1,33},{33,1},{2,34},{34,2},{3,35},{35,3},{4,36},{36... | collective-permute-start | bytes 589832 | tf_op jit(solution)/shard_map/ppermute | solution.py:36
  114.1 26.8 %collective-permute-start.38 = (bf16[4,4,256,256]{3,2,1,0:T(8,128)(2,1)S(1)}, bf16[4,4,256,256]{3,2,1,0:T(8,128)(2,1)S(1)}, u32[]{:S(2)}, u32[]{:S(2)}) collective-permute-start(bf16[4,4,256,256]{3,2,1,0:T(8,128)(2,1)S(1)} %pad_maximum_fusion.refs_8_), channel_id=1, source_target_pairs={{0,32},{32,0},{1,33},{33,1},{2,34},{34,2},{3,35},{35,3},{4,36},{36... | collective-permute-start | bytes 6291464 | tf_op jit(solution)/shard_map/ppermute | solution.py:36
  114.2 8.7 %collective-permute-start.30 = (bf16[256,256]{1,0:T(8,128)(2,1)S(1)}, bf16[256,256]{1,0:T(8,128)(2,1)S(1)}, u32[]{:S(2)}, u32[]{:S(2)}) collective-permute-start(bf16[256,256]{1,0:T(8,128)(2,1)S(1)} %bitcast.53), channel_id=1, source_target_pairs={{0,28},{4,0},{8,4},{12,8},{16,12},{20,16},{24,20},{28,24},{1,29},{... | collective-permute-start | bytes 393224 | tf_op jit(solution)/shard_map/ppermute | solution.py:36
  114.7 8.3 %collective-permute-start.31 = (bf16[256,256]{1,0:T(8,128)(2,1)S(1)}, bf16[256,256]{1,0:T(8,128)(2,1)S(1)}, u32[]{:S(2)}, u32[]{:S(2)}) collective-permute-start(bf16[256,256]{1,0:T(8,128)(2,1)S(1)} %bitcast.54), channel_id=1, source_target_pairs={{0,4},{4,8},{8,12},{12,16},{16,20},{20,24},{24,28},{28,0},{1,5},{5... | collective-permute-start | bytes 393224 | tf_op jit(solution)/shard_map/ppermute | solution.py:36
  116.3 8.4 %collective-permute-start.32 = (bf16[256,256]{1,0:T(8,128)(2,1)S(1)}, bf16[256,256]{1,0:T(8,128)(2,1)S(1)}, u32[]{:S(2)}, u32[]{:S(2)}) collective-permute-start(bf16[256,256]{1,0:T(8,128)(2,1)S(1)} %bitcast.55), channel_id=1, source_target_pairs={{0,24},{4,28},{8,0},{12,4},{16,8},{20,12},{24,16},{28,20},{1,25},{... | collective-permute-start | bytes 393224 | tf_op jit(solution)/shard_map/ppermute | solution.py:36
  117.0 8.3 %collective-permute-start.33 = (bf16[256,256]{1,0:T(8,128)(2,1)S(1)}, bf16[256,256]{1,0:T(8,128)(2,1)S(1)}, u32[]{:S(2)}, u32[]{:S(2)}) collective-permute-start(bf16[256,256]{1,0:T(8,128)(2,1)S(1)} %bitcast.56), channel_id=1, source_target_pairs={{0,8},{4,12},{8,16},{12,20},{16,24},{20,28},{24,0},{28,4},{1,9},{5... | collective-permute-start | bytes 393224 | tf_op jit(solution)/shard_map/ppermute | solution.py:36
  125.3 9.5 %collective-permute-start.36 = (bf16[128,256]{1,0:T(8,128)(2,1)S(1)}, bf16[128,256]{1,0:T(8,128)(2,1)S(1)}, u32[]{:S(2)}, u32[]{:S(2)}) collective-permute-start(bf16[128,256]{1,0:T(8,128)(2,1)S(1)} %slice.34), channel_id=1, source_target_pairs={{0,24},{4,28},{8,0},{12,4},{16,8},{20,12},{24,16},{28,20},{1,25},{... | collective-permute-start | bytes 196616 | tf_op jit(solution)/shard_map/ppermute | solution.py:36
  128.1 7.3 %collective-permute-start.37 = (bf16[128,256]{1,0:T(8,128)(2,1)S(1)}, bf16[128,256]{1,0:T(8,128)(2,1)S(1)}, u32[]{:S(2)}, u32[]{:S(2)}) collective-permute-start(bf16[128,256]{1,0:T(8,128)(2,1)S(1)} %slice.35), channel_id=1, source_target_pairs={{0,8},{4,12},{8,16},{12,20},{16,24},{20,28},{24,0},{28,4},{1,9},{5... | collective-permute-start | bytes 196616 | tf_op jit(solution)/shard_map/ppermute | solution.py:36
  131.0 6.3 %collective-permute-start.34 = (bf16[256,256]{1,0:T(8,128)(2,1)S(1)}, bf16[256,256]{1,0:T(8,128)(2,1)S(1)}, u32[]{:S(2)}, u32[]{:S(2)}) collective-permute-start(bf16[256,256]{1,0:T(8,128)(2,1)S(1)} %collective-permute-done.32.refs_2_), channel_id=1, source_target_pairs={{0,28},{4,0},{8,4},{12,8},{16,12},{20,16},{24,20},{28,24},{1,29},{... | collective-permute-start | bytes 393224 | tf_op jit(solution)/shard_map/ppermute | solution.py:36
  134.7 6.2 %collective-permute-start.35 = (bf16[256,256]{1,0:T(8,128)(2,1)S(1)}, bf16[256,256]{1,0:T(8,128)(2,1)S(1)}, u32[]{:S(2)}, u32[]{:S(2)}) collective-permute-start(bf16[256,256]{1,0:T(8,128)(2,1)S(1)} %collective-permute-done.33.refs_4_), channel_id=1, source_target_pairs={{0,4},{4,8},{8,12},{12,16},{16,20},{20,24},{24,28},{28,0},{1,5},{5... | collective-permute-start | bytes 393224 | tf_op jit(solution)/shard_map/ppermute | solution.py:36
  143.4 6.4 %collective-permute-start.39 = (bf16[256,256]{1,0:T(8,128)(2,1)S(1)}, bf16[256,256]{1,0:T(8,128)(2,1)S(1)}, u32[]{:S(2)}, u32[]{:S(2)}) collective-permute-start(bf16[256,256]{1,0:T(8,128)(2,1)S(1)} %get-tuple-element.115), channel_id=1, source_target_pairs={{0,1},{1,2},{2,3},{3,0},{4,5},{5,6},{6,7},{7,4},{8,9},{9,10},{10,1... | collective-permute-start | bytes 393224 | tf_op jit(solution)/shard_map/ppermute | solution.py:36
  145.8 6.6 %collective-permute-start.40 = (bf16[256,256]{1,0:T(8,128)(2,1)S(1)}, bf16[256,256]{1,0:T(8,128)(2,1)S(1)}, u32[]{:S(2)}, u32[]{:S(2)}) collective-permute-start(bf16[256,256]{1,0:T(8,128)(2,1)S(1)} %get-tuple-element.117), channel_id=1, source_target_pairs={{0,2},{1,3},{2,0},{3,1},{4,6},{5,7},{6,4},{7,5},{8,10},{9,11},{10,... | collective-permute-start | bytes 393224 | tf_op jit(solution)/shard_map/ppermute | solution.py:36
  145.8 7.6 %collective-permute-start.41 = (bf16[256,256]{1,0:T(8,128)(2,1)S(1)}, bf16[256,256]{1,0:T(8,128)(2,1)S(1)}, u32[]{:S(2)}, u32[]{:S(2)}) collective-permute-start(bf16[256,256]{1,0:T(8,128)(2,1)S(1)} %get-tuple-element.116), channel_id=1, source_target_pairs={{0,3},{1,0},{2,1},{3,2},{4,7},{5,4},{6,5},{7,6},{8,11},{9,8},{10,9... | collective-permute-start | bytes 393224 | tf_op jit(solution)/shard_map/ppermute | solution.py:36
  (9 other events, 86.1 us)
